TPU v7x, 128 devices: a whole 4x4x4 slice. The times are simulated.
128 devices in a mesh: grp: 8 (over x_lo, z), tp: 16 (over y, x_hi, core).
Axes of the slice: x: 4 (x_hi: 2, x_lo: 2; x = x_hi * 2 + x_lo), y: 4, z: 4, core: 2. Of those that a mesh axis runs over, the one named last changes fastest.
Arguments:
- activations: bfloat16 [12288, 5120], P('grp', 'tp'), may hold values from -6 to 6
- norm_gain: float32 [5120], replicated, may hold values from 0.1 to 1.9
- query_gain: float32 [128], replicated, may hold values from 0.1 to 1.9
- key_gain: float32 [128], replicated, may hold values from 0.1 to 1.9
- query_weight: bfloat16 [5120, 8192], P('grp', 'tp'), may hold values from -0.078125 to 0.078125
- keyval_weight: bfloat16 [5120, 2048], P('grp', 'tp'), may hold values from -0.078125 to 0.078125
- lengths: int32 [8, 8], replicated, may hold values from 1 to 1529, as said below
Outputs:
- key_value_cache: bfloat16 [12288, 2048], P('grp', 'tp')
- attention_context: bfloat16 [12288, 8192], P('grp', 'tp')
Inputs may be any that keep to these rules, and one draw needn't show every extreme that they name: `lengths`: every length is positive. A group's block of 128 rows (rows k * 128 to (k + 1) * 128 - 1 of the group) is live if it holds a row of one of the group's rollouts. The live blocks of all groups number exactly 48. In one group all 1536 rows are used: one of its rollouts has 1529 rows and the others one row each.
All inputs are finite; a program needn't handle non-finite values.
Results may differ from a plain program's by a relative error of at most 0.0077.
Values may be sent and summed in bfloat16 or wider, within the bound.
A program may use at most 128 MiB of HBM per device.

v0:
```python
import math

import jax
import jax.numpy as jnp
from jax import lax
from jax.sharding import PartitionSpec as P

eps = 1e-06
theta_log = math.log(1000000.0)


def swapped(shard, axis, apart):
    return lax.ppermute(shard, axis, [(i, i ^ 1 << apart) for i in range(lax.axis_size(axis))])


def row_layout(lengths_row, row_ids):
    rollout_ends = jnp.cumsum(lengths_row)
    passed = row_ids[:, None] >= rollout_ends[None, :]
    segment = jnp.sum(passed.astype(jnp.int32), axis=1)
    before = jnp.sum(jnp.where(passed, lengths_row[None, :], 0), axis=1)
    position = row_ids - before
    is_live = segment < lengths_row.shape[0]
    return (segment, position, is_live)


def head_norm(values, gains):
    return values * lax.rsqrt(jnp.mean(values * values, axis=-1, keepdims=True) + eps) * gains


def rotate(values, position):
    half_dim = values.shape[-1] // 2
    inverse = jnp.exp(
        jnp.arange(half_dim, dtype=jnp.float32) * (-2.0 * theta_log / values.shape[-1])
    )
    angles = position.astype(jnp.float32)[:, None] * inverse[None, :]
    cosines = jnp.cos(angles)[:, None, :]
    sines = jnp.sin(angles)[:, None, :]
    lower_half = values[..., :half_dim]
    upper_half = values[..., half_dim:]
    return jnp.concatenate(
        [lower_half * cosines - upper_half * sines, upper_half * cosines + lower_half * sines],
        axis=-1,
    )


def fold_rows(normed, query_weight, pair_weight):
    return (
        jnp.dot(
            normed,
            lax.all_gather(query_weight, "grp", axis=0, tiled=True),
            preferred_element_type=jnp.float32,
        ),
        jnp.dot(
            normed,
            lax.all_gather(pair_weight, "grp", axis=0, tiled=True),
            preferred_element_type=jnp.float32,
        ),
    )


def finish_keyval(keyval_sum, position, is_live, key_gain):
    row_count = keyval_sum.shape[0]
    head_dim = key_gain.shape[0]
    blocks = keyval_sum.reshape(row_count, -1, head_dim)
    keyed = rotate(head_norm(blocks, key_gain), position)
    is_key = (jnp.arange(2) == 0)[None, :, None]
    mixed = jnp.where(is_key, keyed, blocks).astype(jnp.bfloat16)
    return jnp.where(is_live[:, None, None], mixed, 0).reshape(row_count, -1)


def project(
    rows_x, position, is_live, norm_gain, query_gain, key_gain, query_weight, keyval_weight
):
    full_rows = lax.all_gather(rows_x, "tp", axis=1, tiled=True)
    as_float = full_rows.astype(jnp.float32)
    inv_rms = lax.rsqrt(jnp.mean(as_float * as_float, axis=1, keepdims=True) + eps)
    normed = (as_float * inv_rms * norm_gain[None, :]).astype(jnp.bfloat16)
    row_count = normed.shape[0]
    head_dim = query_gain.shape[0]
    parity = lax.axis_index("tp") % 2
    partner = swapped(keyval_weight, "tp", 0)
    pair_weight = jnp.where(
        parity == 0,
        jnp.concatenate([keyval_weight, partner], axis=1),
        jnp.concatenate([partner, keyval_weight], axis=1),
    )
    query_sum, keyval_sum = fold_rows(normed, query_weight, pair_weight)
    keyval = finish_keyval(keyval_sum, position, is_live, key_gain)
    query = rotate(head_norm(query_sum.reshape(row_count, -1, head_dim), query_gain), position)
    return (query.astype(jnp.bfloat16).reshape(row_count, -1), keyval)


def attend(query, key_rows, value_rows, segment, position, is_live):
    row_count, heads, head_dim = query.shape
    block_rows = min(512, row_count)

    def one_block(block_index):
        first_row = block_index * block_rows
        query_rows = lax.dynamic_slice_in_dim(query, first_row, block_rows, 0)
        query_segment = lax.dynamic_slice_in_dim(segment, first_row, block_rows, 0)
        query_position = lax.dynamic_slice_in_dim(position, first_row, block_rows, 0)
        query_live = lax.dynamic_slice_in_dim(is_live, first_row, block_rows, 0)
        scores = jnp.einsum(
            "qhd,kd->qhk", query_rows, key_rows, preferred_element_type=jnp.float32
        ) * (1.0 / math.sqrt(head_dim))
        allowed = (query_segment[:, None] == segment[None, :]) & (
            position[None, :] <= query_position[:, None]
        )
        allowed = (allowed & query_live[:, None] & is_live[None, :])[:, None, :]
        scores = jnp.where(allowed, scores, -1e30)
        row_peak = jnp.max(scores, axis=2, keepdims=True)
        weight = jnp.where(allowed, jnp.exp(scores - row_peak), 0.0)
        denominator = jnp.where(
            query_live[:, None, None], jnp.sum(weight, axis=2, keepdims=True), 1.0
        )
        probability = (weight / denominator).astype(jnp.bfloat16)
        return jnp.einsum(
            "qhk,kd->qhd", probability, value_rows, preferred_element_type=jnp.float32
        ).astype(jnp.bfloat16)

    outputs = lax.map(one_block, jnp.arange(row_count // block_rows))
    return outputs.reshape(row_count, heads * head_dim)


def per_device(activations, norm_gain, query_gain, key_gain, query_weight, keyval_weight, lengths):
    own_rows = activations.shape[0]
    group_index = lax.axis_index("grp")
    segment, position, is_live = row_layout(
        lengths[group_index], jnp.arange(own_rows, dtype=jnp.int32)
    )
    query_cols = query_weight.shape[1]
    query, keyval = project(
        activations, position, is_live, norm_gain, query_gain, key_gain, query_weight, keyval_weight
    )
    head_dim = query_gain.shape[0]
    heads = query_cols // head_dim
    context = attend(
        query.reshape(own_rows, heads, head_dim),
        keyval[:, :head_dim],
        keyval[:, head_dim:],
        segment,
        position,
        is_live,
    )
    own_width = keyval_weight.shape[1]
    cache_start = lax.axis_index("tp") % (2 * head_dim // own_width) * own_width
    own_cache = lax.dynamic_slice_in_dim(keyval, cache_start, own_width, 1)
    return (own_cache, context)


def solution(mesh):
    placed = (P("grp", "tp"), P(), P(), P(), P("grp", "tp"), P("grp", "tp"), P())
    return jax.shard_map(
        per_device,
        mesh=mesh,
        in_specs=placed,
        out_specs=(P("grp", "tp"), P("grp", "tp")),
        check_vma=False,
    )
```

profile of v0, /device:TPU:0, one launch (start us, length us, event | category | flops | bytes accessed | tf_op | source)
XLA Modules:
  0.0 315.8 jit_solution(9384072715437774812)
XLA Ops:
  7.2 0.0 all-gather.4.cloned.1.call-start
  7.2 0.7 all-gather.4.cloned.1.call-update
  7.9 0.0 all-gather.8.cloned.1.call-start
  7.9 0.7 all-gather.8.cloned.1.call-update
  8.6 0.0 all-gather.6.cloned.1.call-start
  8.7 0.1 collective-permute-start
  8.8 0.7 fusion.37
  9.5 0.2 reduce-window.8
  9.7 0.1 convert_reduce_fusion
  9.8 0.5 collective-permute-done
  10.4 1.8 maximum_select_fusion
  12.2 0.0 all-gather.6.cloned.1.call-update
  12.2 1.4 multiply_cosine_fusion
  13.7 1.2 copy.24
  14.8 1.2 copy.25
  16.0 0.6 broadcast_bitcast_fusion
  16.6 0.6 broadcast_compare_fusion
  17.2 100.1 %all-gather.4.cloned.1.call-done = bf16[1536,5120]{0,1:T(8,128)(2,1)} async-done(((bf16[1536,320]{0,1:T(8,128)(2,1)}), bf16[1536,5120]{0,1:T(8,128)(2,1)}) %all-gather.4.cloned.1.call-update) | async-done | bytes 15728656 | tf_op jit(solution)/shard_map/all_gather | solution.py:74
  117.3 7.0 %fusion.28 = f32[1536]{0:T(1024)S(1)} fusion(bf16[1536,5120]{0,1:T(8,128)(2,1)} %all-gather.4.cloned.1.call-done), kind=kLoop, calls=%fused_computation.27 | loop fusion | flops 23591424 | bytes 15734784 | tf_op jit(solution)/shard_map/reduce_sum | solution.py:76
  124.3 55.0 %all-gather.8.cloned.1.call-done = bf16[5120,512]{1,0:T(8,128)(2,1)} async-done(((bf16[640,512]{1,0:T(8,128)(2,1)}), bf16[5120,512]{1,0:T(8,128)(2,1)}) %all-gather.8.cloned.1.call-update) | async-done | bytes 5242896 | tf_op jit(solution)/shard_map/all_gather | solution.py:50
  179.3 15.7 %multiply_reduce_fusion = (f32[1536,4]{0,1:T(4,128)}, f32[1536,512]{0,1:T(8,128)}) fusion(bf16[5120,512]{1,0:T(8,128)(2,1)} %all-gather.8.cloned.1.call-done, bf16[1536,5120]{0,1:T(8,128)(2,1)} %all-gather.4.cloned.1.call-done, f32[5120]{0:T(1024)S(1)} %copy-done.12, f32[1536]{0:T(1024)S(1)} %add_rsqrt_fusion.2), kind=kOutput, calls=%fused_computation.35 | convolution fusion | flops 8086087680 | bytes 24168448 | tf_op jit(solution)/shard_map/dot_general | solution.py:48
  195.1 2.4 copy.23
  197.5 1.4 add_rsqrt_fusion
  198.8 23.2 %all-gather.6.cloned.1.call-done = bf16[5120,256]{1,0:T(8,128)(2,1)} async-done(((bf16[640,256]{1,0:T(8,128)(2,1)}), bf16[5120,256]{1,0:T(8,128)(2,1)}) %all-gather.6.cloned.1.call-update) | async-done | bytes 2621456 | tf_op jit(solution)/shard_map/all_gather | solution.py:55
  222.1 10.8 %multiply_reduce_fusion.1 = (f32[1536,2]{0,1:T(2,128)S(1)}, f32[1536,256]{0,1:T(8,128)S(1)}) fusion(bf16[5120,256]{1,0:T(8,128)(2,1)} %all-gather.6.cloned.1.call-done, bf16[1536,5120]{0,1:T(8,128)(2,1)} %all-gather.4.cloned.1.call-done, f32[5120]{0:T(1024)} %param.10, f32[1536]{0:T(1024)} %copy-done.9), kind=kOutput, calls=%fused_computation.42 | convolution fusion | flops 4058772480 | bytes 19961856 | tf_op jit(solution)/shard_map/dot_general | solution.py:53
  232.9 0.3 multiply_multiply_fusion.1
  233.3 0.6 copy-done.1
  233.9 0.2 multiply_subtract_fusion
  234.1 0.1 pad_maximum_fusion
  234.2 0.4 copy-done.7
  234.6 0.3 fusion.36
  234.8 1.0 fusion.49
  235.8 1.9 copy.27
  237.7 1.9 copy.26
  239.6 0.9 copy.29
  240.6 1.8 multiply_multiply_fusion
  242.4 1.1 subtract_convert_fusion
  243.5 2.0 pad_maximum_fusion.1
  245.6 62.3 %while.10 = (s32[]{:T(128)}, bf16[3,512,4,128]{3,2,1,0:T(4,128)(2,1)S(1)}, s32[3]{0:T(128)S(1)}, s32[1536]{0:T(1024)S(1)}, s32[1536]{0:T(1024)S(1)}, /*index=5*/...) while((s32[]{:T(128)}, ...), condition=%wide.region_9.10_spmd, body=%wide.region_6.9_spmd.sunk | while | flops 1636830720 | bytes 30469844 | solution.py:121
  245.6 0.6 dynamic_slice.48
  246.8 0.1 dynamic_slice.51
  246.9 0.1 dynamic_slice.50
  247.0 0.1 dynamic_slice.49
  247.0 1.2 and_and_fusion.2
  248.2 11.2 %fusion.60 = (f32[512,4]{0,1:T(4,128)S(1)}, f32[512,4,1536]{2,0,1:T(8,128)}) fusion(pred[512,1536]{1,0:T(8,128)(4,1)S(1)} %and_and_fusion.2, bf16[1536,4,128]{2,0,1:T(8,128)(2,1)} %get-tuple-element.213, s32[]{:T(128)S(6)} %select_n.93, bf16[1536,128]{1,0:T(8,128)(2,1)S(1)} %get-tuple-element.214), kind=kOutput, calls=%fused_computation.65.clone.1 | convolution fusion | flops 821036544 | bytes 15081476 | tf_op jit(solution)/shard_map/while/body/eval_jaxpr/sub | solution.py:112
  259.4 6.4 %fusion.61 = bf16[1,512,4,128]{3,1,2,0:T(8,128)(2,1)S(1)} fusion(f32[512,4,1536]{2,0,1:T(8,128)} %get-tuple-element.179, f32[512,4]{0,1:T(4,128)S(1)} %broadcast_select_fusion.2, bf16[1536,128]{1,0:T(8,128)(2,1)S(1)} %get-tuple-element.215), kind=kOutput, calls=%fused_computation.12.clone.1 | convolution fusion | flops 811859968 | bytes 13508608 | tf_op jit(solution)/shard_map/while/body/eval_jaxpr/qhk,kd->qhd/dot_general | solution.py:117
  265.9 0.4 copy_dynamic-update-slice_fusion.2
  266.3 0.6 dynamic_slice.48
  267.6 0.1 dynamic_slice.51
  267.7 0.1 dynamic_slice.50
  267.7 0.1 dynamic_slice.49
  267.8 1.2 and_and_fusion.2
  269.0 11.2 %fusion.60 = (f32[512,4]{0,1:T(4,128)S(1)}, f32[512,4,1536]{2,0,1:T(8,128)}) fusion(pred[512,1536]{1,0:T(8,128)(4,1)S(1)} %and_and_fusion.2, bf16[1536,4,128]{2,0,1:T(8,128)(2,1)} %get-tuple-element.213, s32[]{:T(128)S(6)} %select_n.93, bf16[1536,128]{1,0:T(8,128)(2,1)S(1)} %get-tuple-element.214), kind=kOutput, calls=%fused_computation.65.clone.1 | convolution fusion | flops 821036544 | bytes 15081476 | tf_op jit(solution)/shard_map/while/body/eval_jaxpr/sub | solution.py:112
  280.2 6.4 %fusion.61 = bf16[1,512,4,128]{3,1,2,0:T(8,128)(2,1)S(1)} fusion(f32[512,4,1536]{2,0,1:T(8,128)} %get-tuple-element.179, f32[512,4]{0,1:T(4,128)S(1)} %broadcast_select_fusion.2, bf16[1536,128]{1,0:T(8,128)(2,1)S(1)} %get-tuple-element.215), kind=kOutput, calls=%fused_computation.12.clone.1 | convolution fusion | flops 811859968 | bytes 13508608 | tf_op jit(solution)/shard_map/while/body/eval_jaxpr/qhk,kd->qhd/dot_general | solution.py:117
  286.7 0.4 copy_dynamic-update-slice_fusion.2
  287.1 0.6 dynamic_slice.48
  288.4 0.1 dynamic_slice.51
  288.4 0.1 dynamic_slice.50
  288.5 0.1 dynamic_slice.49
  288.6 1.2 and_and_fusion.2
  289.8 11.2 %fusion.60 = (f32[512,4]{0,1:T(4,128)S(1)}, f32[512,4,1536]{2,0,1:T(8,128)}) fusion(pred[512,1536]{1,0:T(8,128)(4,1)S(1)} %and_and_fusion.2, bf16[1536,4,128]{2,0,1:T(8,128)(2,1)} %get-tuple-element.213, s32[]{:T(128)S(6)} %select_n.93, bf16[1536,128]{1,0:T(8,128)(2,1)S(1)} %get-tuple-element.214), kind=kOutput, calls=%fused_computation.65.clone.1 | convolution fusion | flops 821036544 | bytes 15081476 | tf_op jit(solution)/shard_map/while/body/eval_jaxpr/sub | solution.py:112
  301.0 6.4 %fusion.61 = bf16[1,512,4,128]{3,1,2,0:T(8,128)(2,1)S(1)} fusion(f32[512,4,1536]{2,0,1:T(8,128)} %get-tuple-element.179, f32[512,4]{0,1:T(4,128)S(1)} %broadcast_select_fusion.2, bf16[1536,128]{1,0:T(8,128)(2,1)S(1)} %get-tuple-element.215), kind=kOutput, calls=%fused_computation.12.clone.1 | convolution fusion | flops 811859968 | bytes 13508608 | tf_op jit(solution)/shard_map/while/body/eval_jaxpr/qhk,kd->qhd/dot_general | solution.py:117
  307.4 0.4 copy_dynamic-update-slice_fusion.2
  307.9 1.4 copy.35
  (34 shorter events, 0.1 us)
Async XLA Ops:
  7.2 110.1 %all-gather.4.cloned.1.call-start = ((), (), s32[]{:S(2)}) async-start(), calls=%async_computation | async-start | bytes 16711680 | tf_op jit(solution)/shard_map/all_gather | solution.py:74
  7.9 171.4 %all-gather.8.cloned.1.call-start = ((), (), s32[]{:S(2)}) async-start(), calls=%async_computation.2 | async-start | bytes 5898240 | tf_op jit(solution)/shard_map/all_gather | solution.py:50
  8.6 213.4 %all-gather.6.cloned.1.call-start = ((), (), s32[]{:S(2)}) async-start(), calls=%async_computation.1 | async-start | bytes 2949120 | tf_op jit(solution)/shard_map/all_gather | solution.py:55
  8.7 1.7 collective-permute-start
  13.6 110.7 %copy-start = (f32[1536,64]{0,1:T(8,128)}, f32[1536,64]{0,1:T(8,128)S(1)}, u32[]{:S(2)}) copy-start(f32[1536,64]{0,1:T(8,128)S(1)} %get-tuple-element.113) | copy-start | bytes 1179652
  17.2 162.1 %copy-start.12 = (f32[5120]{0:T(1024)S(1)}, f32[5120]{0:T(1024)}, u32[]{:S(2)}) copy-start(f32[5120]{0:T(1024)} %param.10) | copy-start | bytes 61444
  124.3 70.7 %copy-start.9 = (f32[1536]{0:T(1024)}, f32[1536]{0:T(1024)S(1)}, u32[]{:S(2)}) copy-start(f32[1536]{0:T(1024)S(1)} %add_rsqrt_fusion.2) | copy-start | bytes 18436
  222.1 10.8 %copy-start.11 = (f32[128]{0:T(128)S(1)}, f32[128]{0:T(128)}, u32[]{:S(2)}) copy-start(f32[128]{0:T(128)} %param.12) | copy-start | bytes 1540
  232.9 1.0 copy-start.1
  233.9 0.7 copy-start.7
  233.9 0.7 copy-start.10
  240.5 1.8 copy-start.2
  240.5 1.8 copy-start.3
  243.5 2.1 copy-start.4
  243.5 2.1 copy-start.5
  243.5 2.1 copy-start.6
  243.5 2.0 copy-start.8
Sparse Core Ops, SparseCore 0:
  10.5 106.7 all-gather.3
  118.9 60.3 all-gather.7
  181.0 41.0 all-gather.5
where the time goes:
time: 317 us; the launch traced here: 316 us
  waiting for transfers between devices  180 us (57%)
  matrix products  79.5 us (25%)
  other arithmetic  21.9 us (7%)
  local copies, waits for them, and re-layouts  18 us (6%)
  between operations  14 us (4%)
    all_gather x1, waiting for transfers between devices, project(): full_rows = lax.all_gather(rows_x, 'tp', axis=1, tiled=True)  100 us
    all_gather x1, waiting for transfers between devices, fold_rows(): lax.all_gather(query_weight, 'grp', axis=0, tiled=True)  55 us
    sub x3, matrix products, one_block(): weight = jnp.where(allowed, jnp.exp(scores - row_peak), 0.0)  33.6 us
    all_gather x1, waiting for transfers between devices, fold_rows(): lax.all_gather(pair_weight, 'grp', axis=0, tiled=True)  23.2 us
    dot_general x3, matrix products, one_block(): jnp.einsum('qhk,kd->qhd', probability, value_rows, preferred_element_type...  19.3 us
    dot_general x1, matrix products, fold_rows(): jnp.dot(normed, lax.all_gather(query_weight, 'grp', axis=0, tiled=True),...  15.7 us
    dot_general x1, matrix products, fold_rows(): jnp.dot(normed, lax.all_gather(pair_weight, 'grp', axis=0, tiled=True), p...  10.8 us
    reduce_sum x1, other arithmetic, project(): jnp.mean(as_float * as_float, axis=1, keepdims=True) + eps  7.03 us
  transfers between devices with their start and end apart: 4, of which 4 were waited for; matrix products, arithmetic and copies ran while one was open for 11% of the time, Pallas kernels for 0%

commit v1 on v0

v1 whole, which is shorter than its diff:
```python
import functools
import math

import jax
import jax.numpy as jnp
import numpy as np
from jax import lax
from jax.experimental import pallas as pl
from jax.experimental.pallas import tpu as pltpu
from jax.sharding import PartitionSpec as P

EPS = 1e-06
THETA = 1000000.0
MESH = pl.DeviceIdType.MESH
HD = 128
ROWS = 1536
CH = 128
HALF = CH // 2
NCH = ROWS // CH
FEAT = 640
WROWS = 640
KH = 320
NW = 10
KTILE = 256
T_KV, T_Q01, T_Q23 = 6, 9, 13


def kernel(
    len_ref, x_ref, gain_ref, freq_ref, qg_ref, kg_ref, wq_ref, wkv_ref,
    cache_ref, ctx_ref,
    xbuf, wbuf, pbuf, ss, ssacc, tinv, cosb, sinb, kbuf, vbuf, acc,
    swap_s, swap_r, ss_s, ss_r, loc_s,
    ax_s, ax_r, ay_s, ay_r, ar_s, ar_r, ad_s, ad_r,
    wx_s, wx_r, wz_s, wz_r, wr_s, wr_r, wd_s, wd_r,
):
    g = lax.axis_index("grp")
    t = lax.axis_index("tp")
    core = lax.rem(t, 2)
    chip = t // 2
    xchip = chip + 1 - 2 * lax.rem(chip, 2)

    def chip_of(base, step):
        return lax.rem(base + 2 * step, 8)

    def tp_dev(c, k):
        return (g, c * 2 + k)

    up, down = tp_dev(chip_of(chip, 1), core), tp_dev(chip_of(chip, 3), core)
    across, twin = tp_dev(xchip, core), tp_dev(chip, 1 - core)
    gx = lax.rem(g + 4, 8)

    def ring(base, step):
        return (base // 4) * 4 + lax.rem(lax.rem(base, 4) + step, 4)

    zup, zdown, wacross = (ring(g, 1), t), (ring(g, 3), t), (gx, t)

    bar = pltpu.get_barrier_semaphore()

    def greet(k, c):
        pl.semaphore_signal(bar, inc=1, device_id=(g, lax.rem(t + k, 16)), device_id_type=MESH)
        return c

    lax.fori_loop(1, 16, greet, 0)
    for d in (zup, zdown, wacross):
        pl.semaphore_signal(bar, inc=1, device_id=d, device_id_type=MESH)

    own_w = pl.multiple_of(g * WROWS, WROWS)
    c1 = pltpu.make_async_copy(wq_ref, wbuf.at[pl.ds(own_w, WROWS), pl.ds(2 * HD, 4 * HD)], loc_s.at[0])
    c2 = pltpu.make_async_copy(
        wkv_ref, wbuf.at[pl.ds(own_w, WROWS), pl.ds(pl.multiple_of(core * HD, HD), HD)], loc_s.at[1]
    )
    c1.start()
    c2.start()
    kbuf[...] = jnp.zeros_like(kbuf)
    vbuf[:, :HD] = jnp.zeros((ROWS, HD), jnp.bfloat16)
    vbuf[:, HD:] = jnp.ones((ROWS, HD), jnp.bfloat16)
    pl.semaphore_wait(bar, 18)

    def rcopy(src, dst, s, r, dev):
        return pltpu.make_async_remote_copy(
            src_ref=src, dst_ref=dst, send_sem=s, recv_sem=r, device_id=dev, device_id_type=MESH
        )

    swap = rcopy(x_ref.at[:, 1 - core], pbuf, swap_s, swap_r, twin)
    swap.start()

    def wview(owner, i, part=None):
        j = i // 2
        col = pl.multiple_of(jnp.where(j == 0, core * HD, HD + HD * j), HD)
        row = owner * WROWS + lax.rem(i, 2) * KH
        n = KH
        if part is not None:
            n = KH // 2
            row = row + part * n
        return wbuf.at[pl.ds(pl.multiple_of(row, 32), n), pl.ds(col, HD)]

    def wmsg(owner, i, s, r, dev, part=None):
        v = wview(owner, i, part)
        return rcopy(v, v, s, r, dev)

    def w_x(i, owner):
        return wmsg(owner, i, wx_s.at[i], wx_r.at[i], wacross)

    def w_z(i, cls, d, owner):
        k = cls * 2 + d
        return wmsg(owner, i, wz_s.at[i, k], wz_r.at[i, k], (zup, zdown)[d])

    def w_r(i, cls, d, owner):
        k = cls * 2 + d
        return wmsg(owner, i, wr_s.at[i, k], wr_r.at[i, k], (zup, zdown)[d], part=d)

    def kvview(i, slot, col):
        row = slot * WROWS + i * KH
        return wbuf.at[pl.ds(pl.multiple_of(row, 32), KH), pl.ds(pl.multiple_of(col * HD, HD), HD)]

    def w_d(i, owner, col):
        v = kvview(i, owner, col)
        return rcopy(v, v, wd_s.at[i, owner], wd_r.at[i, owner], twin)

    def w_share(i, owner):
        @pl.when(i < 2)
        def _():
            w_d(i, owner, core).start()

    def w0(i):
        w_x(i, g).start()
        w_z(i, 0, 0, g).start()
        w_z(i, 0, 1, g).start()
        w_share(i, g)

    def w1(i):
        w_x(i, gx).wait_recv()
        w_z(i, 1, 0, gx).start()
        w_z(i, 1, 1, gx).start()
        w_share(i, gx)
        lo, hi = ring(g, 3), ring(g, 1)
        w_z(i, 0, 0, lo).wait_recv()
        w_r(i, 0, 0, lo).start()
        w_share(i, lo)
        w_z(i, 0, 1, hi).wait_recv()
        w_r(i, 0, 1, hi).start()
        w_share(i, hi)

    def w2(i):
        lo, hi = ring(gx, 3), ring(gx, 1)
        w_z(i, 1, 0, lo).wait_recv()
        w_r(i, 1, 0, lo).start()
        w_share(i, lo)
        w_z(i, 1, 1, hi).wait_recv()
        w_r(i, 1, 1, hi).start()
        w_share(i, hi)

    def w3(i):
        for cls, base in ((0, g), (1, gx)):
            far = ring(base, 2)
            w_r(i, cls, 0, far).wait_recv()
            w_r(i, cls, 1, far).wait_recv()
            w_share(i, far)

    def w4(i):
        @pl.when(i < 2)
        def _():
            def one(owner, c):
                w_d(i, owner, 1 - core).wait_recv()
                return c

            lax.fori_loop(0, 8, one, 0)

    def aview(owner, i, k, part=None):
        row = i * CH + k * HALF
        n = HALF
        if part is not None:
            n = HALF // 2
            row = row + part * n
        return xbuf.at[
            pl.ds(pl.multiple_of(row, 32), n), pl.ds(pl.multiple_of(owner * FEAT, FEAT), FEAT)
        ]

    def amsg(owner, i, s, r, dev, part=None, k=None):
        v = aview(owner, i, core if k is None else k, part)
        return rcopy(v, v, s, r, dev)

    def a_x(i, owner):
        return amsg(owner, i, ax_s.at[i], ax_r.at[i], across)

    def a_y(i, cls, d, owner):
        k = cls * 2 + d
        return amsg(owner, i, ay_s.at[i, k], ay_r.at[i, k], (up, down)[d])

    def a_r(i, cls, d, owner):
        k = cls * 2 + d
        return amsg(owner, i, ar_s.at[i, k], ar_r.at[i, k], (up, down)[d], part=d)

    def a_d(i, owner, k):
        return amsg(owner, i, ad_s.at[i, owner], ad_r.at[i, owner], twin, k=k)

    def a0(i):
        a_y(i, 0, 0, chip).start()
        a_y(i, 0, 1, chip).start()
        a_x(i, chip).start()
        a_d(i, chip, core).start()

    def a1(i):
        a_x(i, xchip).wait_recv()
        a_y(i, 1, 0, xchip).start()
        a_y(i, 1, 1, xchip).start()
        a_d(i, xchip, core).start()
        lo, hi = chip_of(chip, 3), chip_of(chip, 1)
        a_y(i, 0, 0, lo).wait_recv()
        a_r(i, 0, 0, lo).start()
        a_d(i, lo, core).start()
        a_y(i, 0, 1, hi).wait_recv()
        a_r(i, 0, 1, hi).start()
        a_d(i, hi, core).start()

    def a2(i):
        lo, hi = chip_of(xchip, 3), chip_of(xchip, 1)
        a_y(i, 1, 0, lo).wait_recv()
        a_r(i, 1, 0, lo).start()
        a_d(i, lo, core).start()
        a_y(i, 1, 1, hi).wait_recv()
        a_r(i, 1, 1, hi).start()
        a_d(i, hi, core).start()

    def a3(i):
        for cls, base in ((0, chip), (1, xchip)):
            far = chip_of(base, 2)
            a_r(i, cls, 0, far).wait_recv()
            a_r(i, cls, 1, far).wait_recv()
            a_d(i, far, core).start()

    def a4(i):
        def one(owner, c):
            a_d(i, owner, 1 - core).wait_recv()
            return c

        lax.fori_loop(0, 8, one, 0)

    own_f = pl.multiple_of(chip * FEAT, FEAT)

    def merge(i):
        mine = x_ref[i, core].astype(jnp.float32)
        other = pbuf[i].astype(jnp.float32)
        first = jnp.where(core == 0, mine, other)
        second = jnp.where(core == 0, other, mine)
        both = jnp.concatenate([first, second], axis=1)
        squares = jnp.sum(both * both, axis=1, keepdims=True)
        scaled = (both * gain_ref[:, pl.ds(own_f, FEAT)]).astype(jnp.bfloat16)
        row = pl.multiple_of(i * CH + core * HALF, 32)
        xbuf[pl.ds(row, HALF), pl.ds(own_f, FEAT)] = scaled
        lane = lax.broadcasted_iota(jnp.int32, (HALF, CH), 1)
        at = pl.ds(pl.multiple_of(core * HALF, HALF), HALF)
        ssacc[at, :] = jnp.where(lane == i, squares, ssacc[at, :])

    ssacc[...] = jnp.zeros_like(ssacc)
    c2.wait()
    c1.wait()
    w0(0)
    w0(1)
    swap.wait_recv()
    merge(0)
    a0(0)
    merge(1)
    a0(1)

    def merge_rest(i, c):
        merge(i)
        return c

    lax.fori_loop(2, NCH, merge_rest, 0)
    ss[t] = jnp.transpose(ssacc[...])[:16]

    def ss_msg(slot, k):
        return rcopy(ss.at[slot], ss.at[slot], ss_s.at[k], ss_r.at[slot], (g, lax.rem(t + k, 16)))

    def ss_go(k, c):
        ss_msg(t, k).start()
        return c

    lax.fori_loop(1, 16, ss_go, 0)

    ends = []
    total = 0
    for r in range(8):
        total = total + len_ref[g, r]
        ends.append(total)

    def starts_of(rows):
        start = jnp.zeros_like(rows)
        for r in range(8):
            start = start + jnp.where(rows >= ends[r], len_ref[g, r], 0)
        return start

    def rows_of(u, n, lanes):
        return u * CH + lax.broadcasted_iota(jnp.int32, (n, lanes), 0)

    def trig(u, c):
        rows = rows_of(u, CH, HD)
        angle = (rows - starts_of(rows)).astype(jnp.float32) * freq_ref[...]
        lane = lax.broadcasted_iota(jnp.int32, (CH, HD), 1)
        at = pl.ds(pl.multiple_of(u * CH, CH), CH)
        cosb[at, :] = jnp.cos(angle)
        sinb[at, :] = jnp.where(lane < HD // 2, -1.0, 1.0) * jnp.sin(angle)
        return c

    lax.fori_loop(0, NCH, trig, 0)

    def at_rows(u):
        return pl.ds(pl.multiple_of(u * CH, CH), CH)

    def inv_of(u):
        lane = lax.broadcasted_iota(jnp.int32, (CH, CH), 1)
        return jnp.sum(jnp.where(lane == u, tinv[...], 0.0), axis=1, keepdims=True)

    def finish(a, inv, gains, u):
        m = jnp.mean(a * a, axis=1, keepdims=True)
        a = a * (inv * lax.rsqrt(inv * inv * m + EPS)) * gains
        return a * cosb[at_rows(u), :] + pltpu.roll(a, HD // 2, 1) * sinb[at_rows(u), :]

    def project(u, col):
        return jnp.dot(
            xbuf[at_rows(u), :], wbuf[:, pl.ds(col, 2 * HD)], preferred_element_type=jnp.float32
        )

    def do_kv(u, c):
        r = project(u, 0)
        inv = inv_of(u)
        live = rows_of(u, CH, HD) < total
        key = jnp.where(live, finish(r[:, :HD], inv, kg_ref[...], u), 0.0).astype(jnp.bfloat16)
        val = jnp.where(live, r[:, HD:] * inv, 0.0).astype(jnp.bfloat16)
        kbuf[at_rows(u), :] = key
        vbuf[at_rows(u), pl.ds(0, HD)] = val
        cache_ref[at_rows(u), :] = jnp.where(core == 0, key, val)
        return c

    def do_q(u, pair):
        r = project(u, 2 * HD + pair * 2 * HD)
        inv = inv_of(u)
        q = jnp.concatenate(
            [finish(r[:, h * HD:(h + 1) * HD], inv, qg_ref[...], u).astype(jnp.bfloat16) for h in range(2)],
            axis=0,
        )
        rows = rows_of(u, CH, KTILE)
        start = starts_of(rows)
        acc[...] = jnp.zeros_like(acc)

        def one(j, c):
            at = pl.ds(pl.multiple_of(j * KTILE, KTILE), KTILE)
            s = lax.dot_general(
                q, kbuf[at, :], (((1,), (1,)), ((), ())), preferred_element_type=jnp.float32
            )
            keys = j * KTILE + lax.broadcasted_iota(jnp.int32, (CH, KTILE), 1)
            allowed = (keys >= start) & (keys <= rows)
            p = jnp.exp(s * (1.0 / math.sqrt(HD)))
            p = jnp.concatenate(
                [jnp.where(allowed, p[h * CH:(h + 1) * CH], 0.0) for h in range(2)], axis=0
            ).astype(jnp.bfloat16)
            acc[...] += jnp.dot(p, vbuf[at, :], preferred_element_type=jnp.float32)
            return c

        lax.fori_loop(0, u // 2 + 1, one, 0)
        out = (acc[:, :HD] / acc[:, HD:]).astype(jnp.bfloat16)
        for h in range(2):
            ctx_ref[at_rows(u), pl.ds((pair * 2 + h) * HD, HD)] = out[h * CH:(h + 1) * CH]

    def do_q01(u, c):
        do_q(u, 0)
        return c

    def do_q23(u, c):
        do_q(u, 1)
        return c

    def stage(k, lo, hi, fn):
        @pl.when((k >= lo) & (k < hi))
        def _():
            fn(k)

    def tick(k, c):
        stage(k, 0, NCH, a0)
        stage(k, 0, NW, w0)
        stage(k - 2, 0, NCH, a1)
        stage(k - 2, 0, NW, w1)
        stage(k - 3, 0, NCH, a2)
        stage(k - 3, 0, NW, w2)
        stage(k - 4, 0, NCH, a3)
        stage(k - 4, 0, NW, w3)
        stage(k - 5, 0, NCH, a4)
        stage(k - 5, 0, NW, w4)

        @pl.when(k == T_KV)
        def _():
            def ss_wait(j, c):
                ss_msg(lax.rem(t + j, 16), j).wait_recv()
                return c

            lax.fori_loop(1, 16, ss_wait, 0)
            sums = jnp.sum(ss[...], axis=0)
            inv = lax.rsqrt(sums * (1.0 / (8 * FEAT)) + EPS)
            tinv[...] = jnp.transpose(jnp.concatenate([inv] * 8, axis=0))

        last = k - 5
        for first, fn in ((T_KV, do_kv), (T_Q01, do_q01), (T_Q23, do_q23)):
            @pl.when(k >= first)
            def _():
                lax.fori_loop(jnp.where(k == first, 0, last), last + 1, fn, 0)

        return c

    lax.fori_loop(2, NCH + 5, tick, 0)

    swap.wait_send()

    def ss_sent(j, c):
        ss_msg(t, j).wait_send()
        return c

    lax.fori_loop(1, 16, ss_sent, 0)

    def w_sent(i, c):
        w_x(i, g).wait_send()
        for cls in range(2):
            for d in range(2):
                w_z(i, cls, d, g).wait_send()
                w_r(i, cls, d, g).wait_send()
        return c

    lax.fori_loop(0, NW, w_sent, 0)

    def wd_sent(n, c):
        w_d(n // 8, lax.rem(n, 8), core).wait_send()
        return c

    lax.fori_loop(0, 16, wd_sent, 0)

    def a_sent(i, c):
        a_x(i, chip).wait_send()
        for cls in range(2):
            for d in range(2):
                a_y(i, cls, d, chip).wait_send()
                a_r(i, cls, d, chip).wait_send()

        def one(owner, c):
            a_d(i, owner, core).wait_send()
            return c

        lax.fori_loop(0, 8, one, 0)
        return c

    lax.fori_loop(0, NCH, a_sent, 0)


def per_device(activations, norm_gain, query_gain, key_gain, query_weight, keyval_weight, lengths):
    half = np.arange(64, dtype=np.float64)
    freq = np.exp(half * (-2.0 * math.log(THETA) / HD)).astype(np.float32)
    freq = jnp.asarray(np.concatenate([freq, freq])[None, :])
    vmem = pl.BlockSpec(memory_space=pltpu.VMEM)
    hbm = pl.BlockSpec(memory_space=pl.ANY)
    dma = pltpu.SemaphoreType.DMA
    bf16, f32 = jnp.bfloat16, jnp.float32
    sems = []
    for shape in ((NCH,), (NCH, 4), (NCH, 4), (NCH, 8), (NW,), (NW, 4), (NW, 4), (2, 8)):
        sems += [dma(shape), dma(shape)]
    return pl.pallas_call(
        kernel,
        out_shape=(
            jax.ShapeDtypeStruct((ROWS, HD), bf16),
            jax.ShapeDtypeStruct((ROWS, 4 * HD), bf16),
        ),
        in_specs=[pl.BlockSpec(memory_space=pltpu.SMEM)] + [vmem] * 5 + [hbm] * 2,
        out_specs=(vmem, vmem),
        scratch_shapes=[
            pltpu.VMEM((ROWS, 8 * FEAT), bf16),
            pltpu.VMEM((8 * WROWS, 6 * HD), bf16),
            pltpu.VMEM((NCH, HALF, FEAT // 2), bf16),
            pltpu.VMEM((16, 16, CH), f32),
            pltpu.VMEM((CH, CH), f32),
            pltpu.VMEM((CH, CH), f32),
            pltpu.VMEM((ROWS, HD), f32),
            pltpu.VMEM((ROWS, HD), f32),
            pltpu.VMEM((ROWS, HD), bf16),
            pltpu.VMEM((ROWS, 2 * HD), bf16),
            pltpu.VMEM((2 * CH, 2 * HD), f32),
            dma, dma, dma((16,)), dma((16,)), dma((2,)),
            *sems,
        ],
        compiler_params=pltpu.CompilerParams(
            collective_id=0, has_side_effects=True, vmem_limit_bytes=56 * 2**20
        ),
        cost_estimate=pl.CostEstimate(
            flops=2 * ROWS * 5120 * 768, bytes_accessed=4 * 2**20, transcendentals=4 * ROWS * ROWS
        ),
    )(
        lengths,
        activations.reshape(NCH, 2, HALF, FEAT // 2),
        norm_gain[None, :],
        freq,
        query_gain[None, :],
        key_gain[None, :],
        query_weight,
        keyval_weight,
    )


def solution(mesh):
    placed = (P("grp", "tp"), P(), P(), P(), P("grp", "tp"), P("grp", "tp"), P())
    return jax.shard_map(
        per_device,
        mesh=mesh,
        in_specs=placed,
        out_specs=(P("grp", "tp"), P("grp", "tp")),
        check_vma=False,
    )
```

time: 317 us -> 133 us (0.42)
  waiting for transfers between devices: 180 us -> 0 us
  Pallas kernels: 0 us -> 126 us
  matrix products: 79.5 us -> 0 us
  other arithmetic: 21.9 us -> 0 us
  between operations: 14 us -> 0.64 us
  local copies, waits for them, and re-layouts: 18 us -> 6.76 us
    all_gather x3 -> x0, waiting for transfers between devices: 178 us -> none  [the longest x1 100 us: project(): full_rows = lax.all_gather(rows_x, 'tp', axis=1, tiled=True)]
    pallas_call x0 -> x1, Pallas kernels: none -> 126 us  [per_device(): pl.pallas_call(kernel, out_shape=(jax.ShapeDtypeStruct((ROWS, HD), bf16),...]
    dot_general x5 -> x0, matrix products: 45.8 us -> none  [the longest x3 19.3 us: one_block(): jnp.einsum('qhk,kd->qhd', probability, value_rows, preferred_element_type...]
    sub x3 -> x0, matrix products: 33.6 us -> none  [one_block(): weight = jnp.where(allowed, jnp.exp(scores - row_peak), 0.0)]
    reduce_sum x2 -> x0, other arithmetic: 7.13 us -> none  [the longest x1 7.03 us: project(): jnp.mean(as_float * as_float, axis=1, keepdims=True) + eps]
    while x2 -> x0, local copies, waits for them, and re-layouts: 3.82 us -> none  [attend(): outputs = lax.map(one_block, jnp.arange(row_count // block_rows))]
    and x3 -> x0, other arithmetic: 3.51 us -> none  [one_block(): allowed = (allowed & query_live[:, None] & is_live[None, :])[:, None, :]]
    unnamed x28 -> x3, local copies, waits for them, and re-layouts: 3.38 us -> 6.76 us
  transfers between devices with their start and end apart: 4 -> 0, of which waited for: 4 -> 0; matrix products, arithmetic and copies ran while one was open for 11% -> 0% of each run, Pallas kernels for 0% -> 0%
where the time goes in v1:
time: 133 us
  Pallas kernels  126 us (95%)
  local copies, waits for them, and re-layouts  6.76 us (5%)
    pallas_call x1, Pallas kernels, per_device(): pl.pallas_call(kernel, out_shape=(jax.ShapeDtypeStruct((ROWS, HD), bf16),...  126 us
    unnamed x3, local copies, waits for them, and re-layouts  6.76 us

profile of v1, /device:TPU:0, one launch (start us, length us, event | category | flops | bytes accessed | tf_op | source)
XLA Modules:
  0.0 133.2 jit_solution(14200073512963152253)
XLA Ops:
  0.6 2.3 %copy.10 = bf16[1536,320]{1,0:T(8,128)(2,1)} copy(bf16[1536,320]{0,1:T(8,128)(2,1)} %param.8) | data formatting | bytes 1966080 | tf_op args[0]
  3.0 125.8 %shard_map.95 = (bf16[1536,128]{1,0:T(8,128)(2,1)}, bf16[1536,512]{1,0:T(8,128)(2,1)}) custom-call(s32[8,8]{1,0:T(8,128)} %len_ref.1, bf16[12,2,64,320]{3,2,1,0:T(8,128)(2,1)} %bitcast.4, f32[1,5120]{1,0:T(1,128)} %bitcast.5, f32[1,128]{1,0:T(1,128)} %constant.2.clone.freq_ref, f32[1,128]{1,0:T(1,128)} %bitcast.6, f32[1,128]{1,0:T(1,128)} %bitcast.7, ...), custom_call_target="tpu_custom_call" | custom-call | flops 12079595520 | bytes 4194304 | tf_op jit(solution)/shard_map/pallas_call | solution.py:464
  128.8 1.8 %copy.13 = bf16[1536,128]{1,0:T(8,128)(2,1)} copy(bf16[1536,128]{1,0:T(8,128)(2,1)} %get-tuple-element.4) | data formatting | bytes 786432
  130.6 2.7 %copy.14 = bf16[1536,512]{1,0:T(8,128)(2,1)} copy(bf16[1536,512]{1,0:T(8,128)(2,1)} %get-tuple-element.5) | data formatting | bytes 3145728

commit v2 on v1

--- a/solution.py
+++ b/solution.py
@@ -22,14 +22,15 @@
 KH = 320
 NW = 10
 KTILE = 256
-T_KV, T_Q01, T_Q23 = 6, 9, 13
+T_KV, T_Q01, T_Q23 = 3, 6, 10
+LOG2E = math.log2(math.e)
 
 
 def kernel(
     len_ref, x_ref, gain_ref, freq_ref, qg_ref, kg_ref, wq_ref, wkv_ref,
     cache_ref, ctx_ref,
-    xbuf, wbuf, pbuf, ss, ssacc, tinv, cosb, sinb, kbuf, vbuf, acc,
-    swap_s, swap_r, ss_s, ss_r, loc_s,
+    xbuf, nbuf, wbuf, pbuf, ss, ssacc, tinv, cosb, sinb, kbuf, vbuf, cacheb, ctxb,
+    out_s, swap_s, swap_r, ss_s, ss_r, loc_s,
     ax_s, ax_r, ay_s, ay_r, ar_s, ar_r, ad_s, ad_r,
     wx_s, wx_r, wz_s, wz_r, wr_s, wr_r, wd_s, wd_r,
 ):
@@ -74,6 +75,34 @@
     kbuf[...] = jnp.zeros_like(kbuf)
     vbuf[:, :HD] = jnp.zeros((ROWS, HD), jnp.bfloat16)
     vbuf[:, HD:] = jnp.ones((ROWS, HD), jnp.bfloat16)
+    ssacc[...] = jnp.zeros_like(ssacc)
+
+    ends = []
+    total = 0
+    for r in range(8):
+        total = total + len_ref[g, r]
+        ends.append(total)
+
+    def starts_of(rows):
+        start = jnp.zeros_like(rows)
+        for r in range(8):
+            start = start + jnp.where(rows >= ends[r], len_ref[g, r], 0)
+        return start
+
+    def rows_of(u, n, lanes):
+        return u * CH + lax.broadcasted_iota(jnp.int32, (n, lanes), 0)
+
+    def trig(u, c):
+        rows = rows_of(u, CH, HD)
+        angle = (rows - starts_of(rows)).astype(jnp.float32) * freq_ref[...]
+        lane = lax.broadcasted_iota(jnp.int32, (CH, HD), 1)
+        at = pl.ds(pl.multiple_of(u * CH, CH), CH)
+        cosb[at, :] = jnp.cos(angle)
+        sinb[at, :] = jnp.where(lane < HD // 2, -1.0, 1.0) * jnp.sin(angle)
+        return c
+
+    lax.fori_loop(0, NCH, trig, 0)
+
     pl.semaphore_wait(bar, 18)
 
     def rcopy(src, dst, s, r, dev):
@@ -81,8 +110,15 @@
             src_ref=src, dst_ref=dst, send_sem=s, recv_sem=r, device_id=dev, device_id_type=MESH
         )
 
-    swap = rcopy(x_ref.at[:, 1 - core], pbuf, swap_s, swap_r, twin)
-    swap.start()
+    def swap(i):
+        src = x_ref.at[pl.ds(pl.multiple_of(i * CH + (1 - core) * HALF, HALF), HALF), :]
+        return rcopy(src, pbuf.at[i], swap_s.at[i], swap_r.at[i], twin)
+
+    def swap_go(i, c):
+        swap(i).start()
+        return c
+
+    lax.fori_loop(0, NCH, swap_go, 0)
 
     def wview(owner, i, part=None):
         j = i // 2
@@ -122,33 +158,29 @@
         def _():
             w_d(i, owner, core).start()
 
+    def w_ahead(i):
+        w_x(i, g).start()
+        w_share(i, g)
+
     def w0(i):
-        w_x(i, g).start()
         w_z(i, 0, 0, g).start()
         w_z(i, 0, 1, g).start()
-        w_share(i, g)
 
     def w1(i):
         w_x(i, gx).wait_recv()
         w_z(i, 1, 0, gx).start()
         w_z(i, 1, 1, gx).start()
         w_share(i, gx)
-        lo, hi = ring(g, 3), ring(g, 1)
-        w_z(i, 0, 0, lo).wait_recv()
-        w_r(i, 0, 0, lo).start()
-        w_share(i, lo)
-        w_z(i, 0, 1, hi).wait_recv()
-        w_r(i, 0, 1, hi).start()
-        w_share(i, hi)
 
     def w2(i):
-        lo, hi = ring(gx, 3), ring(gx, 1)
-        w_z(i, 1, 0, lo).wait_recv()
-        w_r(i, 1, 0, lo).start()
-        w_share(i, lo)
-        w_z(i, 1, 1, hi).wait_recv()
-        w_r(i, 1, 1, hi).start()
-        w_share(i, hi)
+        for cls, base in ((0, g), (1, gx)):
+            lo, hi = ring(base, 3), ring(base, 1)
+            w_z(i, cls, 0, lo).wait_recv()
+            w_r(i, cls, 0, lo).start()
+            w_share(i, lo)
+            w_z(i, cls, 1, hi).wait_recv()
+            w_r(i, cls, 1, hi).start()
+            w_share(i, hi)
 
     def w3(i):
         for cls, base in ((0, g), (1, gx)):
@@ -194,33 +226,29 @@
     def a_d(i, owner, k):
         return amsg(owner, i, ad_s.at[i, owner], ad_r.at[i, owner], twin, k=k)
 
+    def a_ahead(i):
+        a_x(i, chip).start()
+        a_d(i, chip, core).start()
+
     def a0(i):
         a_y(i, 0, 0, chip).start()
         a_y(i, 0, 1, chip).start()
-        a_x(i, chip).start()
-        a_d(i, chip, core).start()
 
     def a1(i):
         a_x(i, xchip).wait_recv()
         a_y(i, 1, 0, xchip).start()
         a_y(i, 1, 1, xchip).start()
         a_d(i, xchip, core).start()
-        lo, hi = chip_of(chip, 3), chip_of(chip, 1)
-        a_y(i, 0, 0, lo).wait_recv()
-        a_r(i, 0, 0, lo).start()
-        a_d(i, lo, core).start()
-        a_y(i, 0, 1, hi).wait_recv()
-        a_r(i, 0, 1, hi).start()
-        a_d(i, hi, core).start()
 
     def a2(i):
-        lo, hi = chip_of(xchip, 3), chip_of(xchip, 1)
-        a_y(i, 1, 0, lo).wait_recv()
-        a_r(i, 1, 0, lo).start()
-        a_d(i, lo, core).start()
-        a_y(i, 1, 1, hi).wait_recv()
-        a_r(i, 1, 1, hi).start()
-        a_d(i, hi, core).start()
+        for cls, base in ((0, chip), (1, xchip)):
+            lo, hi = chip_of(base, 3), chip_of(base, 1)
+            a_y(i, cls, 0, lo).wait_recv()
+            a_r(i, cls, 0, lo).start()
+            a_d(i, lo, core).start()
+            a_y(i, cls, 1, hi).wait_recv()
+            a_r(i, cls, 1, hi).start()
+            a_d(i, hi, core).start()
 
     def a3(i):
         for cls, base in ((0, chip), (1, xchip)):
@@ -239,35 +267,40 @@
     own_f = pl.multiple_of(chip * FEAT, FEAT)
 
     def merge(i):
-        mine = x_ref[i, core].astype(jnp.float32)
+        row = pl.multiple_of(i * CH + core * HALF, 32)
+        mine = x_ref[pl.ds(row, HALF), :].astype(jnp.float32)
+        swap(i).wait_recv()
         other = pbuf[i].astype(jnp.float32)
         first = jnp.where(core == 0, mine, other)
         second = jnp.where(core == 0, other, mine)
         both = jnp.concatenate([first, second], axis=1)
         squares = jnp.sum(both * both, axis=1, keepdims=True)
-        scaled = (both * gain_ref[:, pl.ds(own_f, FEAT)]).astype(jnp.bfloat16)
-        row = pl.multiple_of(i * CH + core * HALF, 32)
-        xbuf[pl.ds(row, HALF), pl.ds(own_f, FEAT)] = scaled
+        xbuf[pl.ds(row, HALF), pl.ds(own_f, FEAT)] = both.astype(jnp.bfloat16)
         lane = lax.broadcasted_iota(jnp.int32, (HALF, CH), 1)
         at = pl.ds(pl.multiple_of(core * HALF, HALF), HALF)
         ssacc[at, :] = jnp.where(lane == i, squares, ssacc[at, :])
 
-    ssacc[...] = jnp.zeros_like(ssacc)
+    merge(0)
+    a_ahead(0)
+    a0(0)
     c2.wait()
     c1.wait()
+    w_ahead(0)
     w0(0)
+    merge(1)
+    a_ahead(1)
+    merge(2)
+    a_ahead(2)
+    w_ahead(1)
     w0(1)
-    swap.wait_recv()
-    merge(0)
-    a0(0)
-    merge(1)
-    a0(1)
+    w_ahead(2)
+    w_ahead(3)
 
     def merge_rest(i, c):
         merge(i)
         return c
 
-    lax.fori_loop(2, NCH, merge_rest, 0)
+    lax.fori_loop(3, NCH, merge_rest, 0)
     ss[t] = jnp.transpose(ssacc[...])[:16]
 
     def ss_msg(slot, k):
@@ -278,32 +311,6 @@
         return c
 
     lax.fori_loop(1, 16, ss_go, 0)
-
-    ends = []
-    total = 0
-    for r in range(8):
-        total = total + len_ref[g, r]
-        ends.append(total)
-
-    def starts_of(rows):
-        start = jnp.zeros_like(rows)
-        for r in range(8):
-            start = start + jnp.where(rows >= ends[r], len_ref[g, r], 0)
-        return start
-
-    def rows_of(u, n, lanes):
-        return u * CH + lax.broadcasted_iota(jnp.int32, (n, lanes), 0)
-
-    def trig(u, c):
-        rows = rows_of(u, CH, HD)
-        angle = (rows - starts_of(rows)).astype(jnp.float32) * freq_ref[...]
-        lane = lax.broadcasted_iota(jnp.int32, (CH, HD), 1)
-        at = pl.ds(pl.multiple_of(u * CH, CH), CH)
-        cosb[at, :] = jnp.cos(angle)
-        sinb[at, :] = jnp.where(lane < HD // 2, -1.0, 1.0) * jnp.sin(angle)
-        return c
-
-    lax.fori_loop(0, NCH, trig, 0)
 
     def at_rows(u):
         return pl.ds(pl.multiple_of(u * CH, CH), CH)
@@ -312,56 +319,70 @@
         lane = lax.broadcasted_iota(jnp.int32, (CH, CH), 1)
         return jnp.sum(jnp.where(lane == u, tinv[...], 0.0), axis=1, keepdims=True)
 
-    def finish(a, inv, gains, u):
+    def finish(a, gains, u):
         m = jnp.mean(a * a, axis=1, keepdims=True)
-        a = a * (inv * lax.rsqrt(inv * inv * m + EPS)) * gains
+        a = a * lax.rsqrt(m + EPS) * gains
         return a * cosb[at_rows(u), :] + pltpu.roll(a, HD // 2, 1) * sinb[at_rows(u), :]
 
     def project(u, col):
         return jnp.dot(
-            xbuf[at_rows(u), :], wbuf[:, pl.ds(col, 2 * HD)], preferred_element_type=jnp.float32
+            nbuf[at_rows(u), :], wbuf[:, pl.ds(col, 2 * HD)], preferred_element_type=jnp.float32
         )
 
+    def cache_out(u):
+        return pltpu.make_async_copy(cacheb.at[at_rows(u), :], cache_ref.at[at_rows(u), :], out_s.at[u, 2])
+
+    def ctx_out(u, pair):
+        cols = pl.ds(pl.multiple_of(pair * 2 * HD, 2 * HD), 2 * HD)
+        return pltpu.make_async_copy(ctxb.at[at_rows(u), cols], ctx_ref.at[at_rows(u), cols], out_s.at[u, pair])
+
     def do_kv(u, c):
+        inv = inv_of(u)
+
+        def norm(f, c):
+            cols = pl.ds(pl.multiple_of(f * FEAT, FEAT), FEAT)
+            x = xbuf[at_rows(u), cols].astype(jnp.float32)
+            nbuf[at_rows(u), cols] = (x * inv * gain_ref[:, cols]).astype(jnp.bfloat16)
+            return c
+
+        lax.fori_loop(0, 8, norm, 0)
         r = project(u, 0)
-        inv = inv_of(u)
         live = rows_of(u, CH, HD) < total
-        key = jnp.where(live, finish(r[:, :HD], inv, kg_ref[...], u), 0.0).astype(jnp.bfloat16)
-        val = jnp.where(live, r[:, HD:] * inv, 0.0).astype(jnp.bfloat16)
+        key = jnp.where(live, finish(r[:, :HD], kg_ref[...], u), 0.0).astype(jnp.bfloat16)
+        val = jnp.where(live, r[:, HD:], 0.0).astype(jnp.bfloat16)
         kbuf[at_rows(u), :] = key
         vbuf[at_rows(u), pl.ds(0, HD)] = val
-        cache_ref[at_rows(u), :] = jnp.where(core == 0, key, val)
+        cacheb[at_rows(u), :] = jnp.where(core == 0, key, val)
+        cache_out(u).start()
         return c
 
     def do_q(u, pair):
-        r = project(u, 2 * HD + pair * 2 * HD)
-        inv = inv_of(u)
+        r = project(u, pl.multiple_of(2 * HD + pair * 2 * HD, 2 * HD))
         q = jnp.concatenate(
-            [finish(r[:, h * HD:(h + 1) * HD], inv, qg_ref[...], u).astype(jnp.bfloat16) for h in range(2)],
+            [finish(r[:, h * HD:(h + 1) * HD], qg_ref[...], u).astype(jnp.bfloat16) for h in range(2)],
             axis=0,
         )
-        rows = rows_of(u, CH, KTILE)
-        start = starts_of(rows)
-        acc[...] = jnp.zeros_like(acc)
-
-        def one(j, c):
-            at = pl.ds(pl.multiple_of(j * KTILE, KTILE), KTILE)
+
+        def attend(n):
+            rows = rows_of(u, CH, n)
+            start = starts_of(rows_of(u, CH, HD))[:, :1]
+            keys = lax.broadcasted_iota(jnp.int32, (CH, n), 1)
+            allowed = (keys >= start) & (keys <= rows)
             s = lax.dot_general(
-                q, kbuf[at, :], (((1,), (1,)), ((), ())), preferred_element_type=jnp.float32
+                q, kbuf[:n, :], (((1,), (1,)), ((), ())), preferred_element_type=jnp.float32
             )
-            keys = j * KTILE + lax.broadcasted_iota(jnp.int32, (CH, KTILE), 1)
-            allowed = (keys >= start) & (keys <= rows)
-            p = jnp.exp(s * (1.0 / math.sqrt(HD)))
+            p = jnp.exp2(s * (LOG2E / math.sqrt(HD)))
             p = jnp.concatenate(
                 [jnp.where(allowed, p[h * CH:(h + 1) * CH], 0.0) for h in range(2)], axis=0
             ).astype(jnp.bfloat16)
-            acc[...] += jnp.dot(p, vbuf[at, :], preferred_element_type=jnp.float32)
-            return c
-
-        lax.fori_loop(0, u // 2 + 1, one, 0)
-        out = (acc[:, :HD] / acc[:, HD:]).astype(jnp.bfloat16)
-        for h in range(2):
-            ctx_ref[at_rows(u), pl.ds((pair * 2 + h) * HD, HD)] = out[h * CH:(h + 1) * CH]
+            a = jnp.dot(p, vbuf[:n, :], preferred_element_type=jnp.float32)
+            out = (a[:, :HD] / a[:, HD:]).astype(jnp.bfloat16)
+            for h in range(2):
+                cols = pl.ds(pl.multiple_of((pair * 2 + h) * HD, HD), HD)
+                ctxb[at_rows(u), cols] = out[h * CH:(h + 1) * CH]
+
+        lax.switch(u // 2, [functools.partial(attend, KTILE * (b + 1)) for b in range(ROWS // KTILE)])
+        ctx_out(u, pair).start()
 
     def do_q01(u, c):
         do_q(u, 0)
@@ -377,16 +398,18 @@
             fn(k)
 
     def tick(k, c):
-        stage(k, 0, NCH, a0)
-        stage(k, 0, NW, w0)
-        stage(k - 2, 0, NCH, a1)
-        stage(k - 2, 0, NW, w1)
-        stage(k - 3, 0, NCH, a2)
-        stage(k - 3, 0, NW, w2)
-        stage(k - 4, 0, NCH, a3)
-        stage(k - 4, 0, NW, w3)
-        stage(k - 5, 0, NCH, a4)
-        stage(k - 5, 0, NW, w4)
+        stage(k + 3, 3, NCH, a_ahead)
+        stage(k + 1, 1, NCH, a0)
+        stage(k + 4, 4, NW, w_ahead)
+        stage(k + 2, 2, NW, w0)
+        stage(k, 0, NCH, a1)
+        stage(k + 1, 1, NW, w1)
+        stage(k - 1, 0, NCH, a2)
+        stage(k, 0, NW, w2)
+        stage(k - 2, 0, NCH, a3)
+        stage(k - 1, 0, NW, w3)
+        stage(k - 3, 0, NCH, a4)
+        stage(k - 2, 0, NW, w4)
 
         @pl.when(k == T_KV)
         def _():
@@ -399,17 +422,17 @@
             inv = lax.rsqrt(sums * (1.0 / (8 * FEAT)) + EPS)
             tinv[...] = jnp.transpose(jnp.concatenate([inv] * 8, axis=0))
 
-        last = k - 5
+        last = k - 3
         for first, fn in ((T_KV, do_kv), (T_Q01, do_q01), (T_Q23, do_q23)):
+
             @pl.when(k >= first)
             def _():
                 lax.fori_loop(jnp.where(k == first, 0, last), last + 1, fn, 0)
 
         return c
 
-    lax.fori_loop(2, NCH + 5, tick, 0)
-
-    swap.wait_send()
+    w1(0)
+    lax.fori_loop(0, NCH + 3, tick, 0)
 
     def ss_sent(j, c):
         ss_msg(t, j).wait_send()
@@ -445,9 +468,26 @@
             return c
 
         lax.fori_loop(0, 8, one, 0)
+        swap(i).wait_send()
+        cache_out(i).wait()
+        ctx_out(i, 0).wait()
+        ctx_out(i, 1).wait()
         return c
 
     lax.fori_loop(0, NCH, a_sent, 0)
+
+
+def hand_on(cache_in, ctx_in, cache_ref, ctx_ref, sem):
+    part = ROWS // 4
+    copies = []
+    for n in range(4):
+        rows = pl.ds(n * part, part)
+        copies.append(pltpu.make_async_copy(cache_in.at[rows, :], cache_ref.at[rows, :], sem.at[2 * n]))
+        copies.append(pltpu.make_async_copy(ctx_in.at[rows, :], ctx_ref.at[rows, :], sem.at[2 * n + 1]))
+    for c in copies:
+        c.start()
+    for c in copies:
+        c.wait()
 
 
 def per_device(activations, norm_gain, query_gain, key_gain, query_weight, keyval_weight, lengths):
@@ -461,15 +501,16 @@
     sems = []
     for shape in ((NCH,), (NCH, 4), (NCH, 4), (NCH, 8), (NW,), (NW, 4), (NW, 4), (2, 8)):
         sems += [dma(shape), dma(shape)]
-    return pl.pallas_call(
+    cache, context = pl.pallas_call(
         kernel,
         out_shape=(
             jax.ShapeDtypeStruct((ROWS, HD), bf16),
             jax.ShapeDtypeStruct((ROWS, 4 * HD), bf16),
         ),
         in_specs=[pl.BlockSpec(memory_space=pltpu.SMEM)] + [vmem] * 5 + [hbm] * 2,
-        out_specs=(vmem, vmem),
+        out_specs=(hbm, hbm),
         scratch_shapes=[
+            pltpu.VMEM((ROWS, 8 * FEAT), bf16),
             pltpu.VMEM((ROWS, 8 * FEAT), bf16),
             pltpu.VMEM((8 * WROWS, 6 * HD), bf16),
             pltpu.VMEM((NCH, HALF, FEAT // 2), bf16),
@@ -480,8 +521,9 @@
             pltpu.VMEM((ROWS, HD), f32),
             pltpu.VMEM((ROWS, HD), bf16),
             pltpu.VMEM((ROWS, 2 * HD), bf16),
-            pltpu.VMEM((2 * CH, 2 * HD), f32),
-            dma, dma, dma((16,)), dma((16,)), dma((2,)),
+            pltpu.VMEM((ROWS, HD), bf16),
+            pltpu.VMEM((ROWS, 4 * HD), bf16),
+            dma((NCH, 3)), dma((NCH,)), dma((NCH,)), dma((16,)), dma((16,)), dma((2,)),
             *sems,
         ],
         compiler_params=pltpu.CompilerParams(
@@ -492,7 +534,7 @@
         ),
     )(
         lengths,
-        activations.reshape(NCH, 2, HALF, FEAT // 2),
+        activations,
         norm_gain[None, :],
         freq,
         query_gain[None, :],
@@ -500,6 +542,16 @@
         query_weight,
         keyval_weight,
     )
+    return pl.pallas_call(
+        hand_on,
+        out_shape=(
+            jax.ShapeDtypeStruct((ROWS, HD), bf16),
+            jax.ShapeDtypeStruct((ROWS, 4 * HD), bf16),
+        ),
+        in_specs=[hbm] * 2,
+        out_specs=(hbm, hbm),
+        scratch_shapes=[dma((8,))],
+    )(cache, context)
 
 
 def solution(mesh):

time: 133 us -> 180 us (1.35)
  Pallas kernels: 126 us -> 177 us
  local copies, waits for them, and re-layouts: 6.76 us -> 2.34 us
    pallas_call x0 -> x1, Pallas kernels: none -> 60.7 us  [per_device(): pl.pallas_call(hand_on, out_shape=(jax.ShapeDtypeStruct((ROWS, HD), bf16)...]
    pallas_call x1, Pallas kernels: 126 us -> 116 us  [per_device(): pl.pallas_call(kernel, out_shape=(jax.ShapeDtypeStruct((ROWS, HD), bf16),...]
    unnamed x3 -> x1, local copies, waits for them, and re-layouts: 6.76 us -> 2.34 us
where the time goes in v2:
time: 180 us
  Pallas kernels  177 us (98%)
  local copies, waits for them, and re-layouts  2.34 us (1%)
    pallas_call x1, Pallas kernels, per_device(): pl.pallas_call(kernel, out_shape=(jax.ShapeDtypeStruct((ROWS, HD), bf16),...  116 us
    pallas_call x1, Pallas kernels, per_device(): pl.pallas_call(hand_on, out_shape=(jax.ShapeDtypeStruct((ROWS, HD), bf16)...  60.7 us

profile of v2, /device:TPU:0, one launch (start us, length us, event | category | flops | bytes accessed | tf_op | source)
XLA Modules:
  0.0 179.6 jit_solution(10339147937511477108)
XLA Ops:
  0.6 2.3 %copy.10.x_ref = bf16[1536,320]{1,0:T(8,128)(2,1)} copy(bf16[1536,320]{0,1:T(8,128)(2,1)} %param.8) | data formatting | bytes 1966080 | tf_op args[0]
  3.0 115.9 %shard_map.95 = (bf16[1536,128]{1,0:T(8,128)(2,1)}, bf16[1536,512]{1,0:T(8,128)(2,1)}) custom-call(s32[8,8]{1,0:T(8,128)} %len_ref.1, bf16[1536,320]{1,0:T(8,128)(2,1)} %copy.10.x_ref, f32[1,5120]{1,0:T(1,128)} %bitcast.3, f32[1,128]{1,0:T(1,128)} %constant.2.clone.freq_ref, f32[1,128]{1,0:T(1,128)} %bitcast.4, f32[1,128]{1,0:T(1,128)} %bitcast.5, ...), custom_call_target="tpu_custom_call" | custom-call | flops 12079595520 | bytes 4194304 | tf_op jit(solution)/shard_map/pallas_call | solution.py:504
  118.8 60.7 %shard_map.96 = (bf16[1536,128]{1,0:T(8,128)(2,1)}, bf16[1536,512]{1,0:T(8,128)(2,1)}) custom-call(bf16[1536,128]{1,0:T(8,128)(2,1)} %get-tuple-element.4.cache_in, bf16[1536,512]{1,0:T(8,128)(2,1)} %get-tuple-element.5.ctx_in), custom_call_target="tpu_custom_call" | custom-call | tf_op jit(solution)/shard_map/pallas_call | solution.py:545

commit v3 on v2

v3 whole, which is shorter than its diff:
```python
import functools
import math

import jax
import jax.numpy as jnp
import numpy as np
from jax import lax
from jax.experimental import pallas as pl
from jax.experimental.pallas import tpu as pltpu
from jax.sharding import PartitionSpec as P

EPS = 1e-06
THETA = 1000000.0
MESH = pl.DeviceIdType.MESH
HD = 128
ROWS = 1536
CH = 128
NCH = ROWS // CH
FEAT = 320
WROWS = 640
KH = 320
NW = 10
KTILE = 256
T_KV, T_Q01, T_Q23 = 3, 5, 8
LEAD = 3
LOG2E = math.log2(math.e)


def kernel(
    len_ref, x_ref, gain_ref, freq_ref, qg_ref, kg_ref, wq_ref, wkv_ref,
    cache_ref, ctx_ref,
    xbuf, nbuf, wbuf, gcol, ss, tinv, cosb, sinb, kbuf, vbuf, cacheb, ctxb,
    out_s, ss_s, ss_r, loc_s, a_s, a_r, w_s, w_r,
):
    g = lax.axis_index("grp")
    t = lax.axis_index("tp")
    core = lax.rem(t, 2)
    chip = t // 2
    xchip = chip + 1 - 2 * lax.rem(chip, 2)

    def chip_of(base, step):
        return lax.rem(base + 2 * step, 8)

    def tp_dev(c, k):
        return (g, c * 2 + k)

    up, down = tp_dev(chip_of(chip, 1), core), tp_dev(chip_of(chip, 3), core)
    across, twin = tp_dev(xchip, core), tp_dev(chip, 1 - core)
    gx = lax.rem(g + 4, 8)

    def ring(base, step):
        return (base // 4) * 4 + lax.rem(lax.rem(base, 4) + step, 4)

    zup, zdown, wacross = (ring(g, 1), t), (ring(g, 3), t), (gx, t)

    bar = pltpu.get_barrier_semaphore()

    def greet(k, c):
        pl.semaphore_signal(bar, inc=1, device_id=(g, lax.rem(t + k, 16)), device_id_type=MESH)
        return c

    lax.fori_loop(1, 16, greet, 0)
    for d in (zup, zdown, wacross):
        pl.semaphore_signal(bar, inc=1, device_id=d, device_id_type=MESH)

    own_w = pl.multiple_of(g * WROWS, WROWS)
    c1 = pltpu.make_async_copy(wq_ref, wbuf.at[pl.ds(own_w, WROWS), pl.ds(2 * HD, 4 * HD)], loc_s.at[0])
    c2 = pltpu.make_async_copy(
        wkv_ref, wbuf.at[pl.ds(own_w, WROWS), pl.ds(pl.multiple_of(core * HD, HD), HD)], loc_s.at[1]
    )
    c1.start()
    c2.start()
    own_f = pl.multiple_of(t * FEAT, FEAT)
    ss[t] = jnp.zeros((16, CH), jnp.float32)

    def stage_own(i, c):
        cols = pl.ds(pl.multiple_of(i * CH, CH), CH)
        mine = x_ref[:, cols]
        xbuf[pl.ds(own_f, FEAT), cols] = mine
        mine = mine.astype(jnp.float32)
        ss[t, pl.ds(i, 1), :] = jnp.sum(mine * mine, axis=0, keepdims=True)
        return c

    lax.fori_loop(0, NCH, stage_own, 0)


    ends = []
    total = 0
    for r in range(8):
        total = total + len_ref[g, r]
        ends.append(total)

    def starts_of(rows):
        start = jnp.zeros_like(rows)
        for r in range(8):
            start = start + jnp.where(rows >= ends[r], len_ref[g, r], 0)
        return start

    def rows_of(u, n, lanes):
        return u * CH + lax.broadcasted_iota(jnp.int32, (n, lanes), 0)

    def trig(u, c):
        rows = rows_of(u, CH, HD)
        angle = (rows - starts_of(rows)).astype(jnp.float32) * freq_ref[...]
        lane = lax.broadcasted_iota(jnp.int32, (CH, HD), 1)
        at = pl.ds(pl.multiple_of(u * CH, CH), CH)
        cosb[at, :] = jnp.cos(angle)
        sinb[at, :] = jnp.where(lane < HD // 2, -1.0, 1.0) * jnp.sin(angle)
        return c


    def gain_column(f, c):
        at = pl.ds(pl.multiple_of(f * HD, HD), HD)
        gcol[at, :] = jnp.transpose(jnp.broadcast_to(gain_ref[:, at], (HD, HD)))
        return c

    pl.semaphore_wait(bar, 18)

    def rcopy(src, dst, s, r, dev):
        return pltpu.make_async_remote_copy(
            src_ref=src, dst_ref=dst, send_sem=s, recv_sem=r, device_id=dev, device_id_type=MESH
        )

    def wview(owner, i, part=None):
        j = i // 2
        col = pl.multiple_of(jnp.where(j == 0, core * HD, HD + HD * j), HD)
        row = owner * WROWS + lax.rem(i, 2) * KH
        n = KH
        if part is not None:
            n = KH // 2
            row = row + part * n
        return wbuf.at[pl.ds(pl.multiple_of(row, 32), n), pl.ds(col, HD)]

    def wmsg(owner, i, s, r, dev, part=None):
        v = wview(owner, i, part)
        return rcopy(v, v, s, r, dev)

    def w_x(i, owner):
        return wmsg(owner, i, w_s.at[i], w_r.at[i, 0], wacross)

    def w_z(i, cls, d, owner):
        return wmsg(owner, i, w_s.at[i], w_r.at[i, 1 + cls], (zup, zdown)[d])

    def w_r_(i, cls, d, owner):
        return wmsg(owner, i, w_s.at[i], w_r.at[i, 3 + cls], (zup, zdown)[d], part=d)

    def w_got(i, k, n):
        v = wbuf.at[pl.ds(0, n * KH), pl.ds(0, HD)]
        rcopy(v, v, w_s.at[i], w_r.at[i, k], wacross).wait_recv()

    def kvview(i, slot, col):
        row = slot * WROWS + i * KH
        return wbuf.at[pl.ds(pl.multiple_of(row, 32), KH), pl.ds(pl.multiple_of(col * HD, HD), HD)]

    def w_d(i, owner, col):
        v = kvview(i, owner, col)
        return rcopy(v, v, w_s.at[i], w_r.at[i, 5], twin)

    def w_share(i, owner):
        @pl.when(i < 2)
        def _():
            w_d(i, owner, core).start()

    def w_ahead(i):
        w_x(i, g).start()
        w_share(i, g)

    def w0(i):
        w_z(i, 0, 0, g).start()
        w_z(i, 0, 1, g).start()

    def mixed(i):
        return (i >= 2) & (lax.rem(i, 2) == 0)

    def w_f(i, n, owner):
        return wmsg(owner, i, w_s.at[i], w_r.at[i, (2, 2, 4)[n]], wacross)

    def w1(i):
        w_got(i, 0, 1)

        @pl.when(jnp.logical_not(mixed(i)))
        def _():
            w_z(i, 1, 0, gx).start()
            w_z(i, 1, 1, gx).start()

        w_share(i, gx)

    def w2(i):
        def near(cls, base):
            lo, hi = ring(base, 3), ring(base, 1)
            w_got(i, 1 + cls, 2)
            w_r_(i, cls, 0, lo).start()
            w_r_(i, cls, 1, hi).start()
            w_share(i, lo)
            w_share(i, hi)

        near(0, g)

        @pl.when(mixed(i))
        def _():
            w_f(i, 0, ring(g, 3)).start()
            w_f(i, 1, ring(g, 1)).start()

        @pl.when(jnp.logical_not(mixed(i)))
        def _():
            near(1, gx)

    def w3(i):
        w_got(i, 3, 1)
        w_share(i, ring(g, 2))

        @pl.when(mixed(i))
        def _():
            w_f(i, 2, ring(g, 2)).start()

        @pl.when(jnp.logical_not(mixed(i)))
        def _():
            w_got(i, 4, 1)
            w_share(i, ring(gx, 2))

    def w4(i):
        @pl.when(i < 2)
        def _():
            w_got(i, 5, 8)

        @pl.when(mixed(i))
        def _():
            w_got(i, 2, 2)
            w_got(i, 4, 1)

    def aview(owner, i, k, part=None):
        row = (owner * 2 + k) * FEAT
        n = FEAT
        if part is not None:
            n = FEAT // 2
            row = row + part * n
        return xbuf.at[pl.ds(pl.multiple_of(row, 32), n), pl.ds(pl.multiple_of(i * CH, CH), CH)]

    def amsg(owner, i, s, r, dev, part=None, k=None):
        v = aview(owner, i, core if k is None else k, part)
        return rcopy(v, v, s, r, dev)

    def a_x(i, owner):
        return amsg(owner, i, a_s.at[i], a_r.at[i, 0], across)

    def a_y(i, cls, d, owner):
        return amsg(owner, i, a_s.at[i], a_r.at[i, 1 + cls], (up, down)[d])

    def a_r_(i, cls, d, owner):
        return amsg(owner, i, a_s.at[i], a_r.at[i, 3 + cls], (up, down)[d], part=d)

    def a_d(i, owner, k):
        return amsg(owner, i, a_s.at[i], a_r.at[i, 5], twin, k=k)

    def a_got(i, k, n):
        v = xbuf.at[pl.ds(0, n * FEAT), pl.ds(0, CH)]
        rcopy(v, v, a_s.at[i], a_r.at[i, k], across).wait_recv()

    def a_ahead(i):
        a_x(i, chip).start()
        a_d(i, chip, core).start()

    def a0(i):
        a_y(i, 0, 0, chip).start()
        a_y(i, 0, 1, chip).start()

    def a1(i):
        a_got(i, 0, 1)
        a_y(i, 1, 0, xchip).start()
        a_y(i, 1, 1, xchip).start()
        a_d(i, xchip, core).start()

    def a2(i):
        for cls, base in ((0, chip), (1, xchip)):
            lo, hi = chip_of(base, 3), chip_of(base, 1)
            a_got(i, 1 + cls, 2)
            a_r_(i, cls, 0, lo).start()
            a_r_(i, cls, 1, hi).start()
            a_d(i, lo, core).start()
            a_d(i, hi, core).start()

    def a3(i):
        for cls, base in ((0, chip), (1, xchip)):
            a_got(i, 3 + cls, 1)
            a_d(i, chip_of(base, 2), core).start()

    def a4(i):
        a_got(i, 5, 8)

    for i in range(LEAD):
        a0(i)
        a_ahead(i)
    c2.wait()
    c1.wait()
    for i in range(LEAD):
        w_ahead(i)
        w0(i)

    def ss_msg(slot, k):
        return rcopy(ss.at[slot], ss.at[slot], ss_s, ss_r, (g, lax.rem(t + k, 16)))

    def ss_go(k, c):
        ss_msg(t, k).start()
        return c

    lax.fori_loop(1, 16, ss_go, 0)

    def at_rows(u):
        return pl.ds(pl.multiple_of(u * CH, CH), CH)

    def finish(a, gains, u):
        m = jnp.mean(a * a, axis=1, keepdims=True)
        a = a * lax.rsqrt(m + EPS) * gains
        return a * cosb[at_rows(u), :] + pltpu.roll(a, HD // 2, 1) * sinb[at_rows(u), :]

    def project(u, col):
        return lax.dot_general(
            nbuf[:, at_rows(u)],
            wbuf[:, pl.ds(col, 2 * HD)],
            (((0,), (0,)), ((), ())),
            preferred_element_type=jnp.float32,
        )

    def cache_out(u):
        return pltpu.make_async_copy(cacheb.at[at_rows(u), :], cache_ref.at[at_rows(u), :], out_s.at[0])

    def ctx_out(u, pair):
        cols = pl.ds(pl.multiple_of(pair * 2 * HD, 2 * HD), 2 * HD)
        return pltpu.make_async_copy(ctxb.at[at_rows(u), cols], ctx_ref.at[at_rows(u), cols], out_s.at[1])

    def do_kv(u, c):
        inv = tinv[pl.ds(u, 1), :]

        def norm(f, c):
            rows = pl.ds(pl.multiple_of(f * 2 * FEAT, 2 * FEAT), 2 * FEAT)
            x = xbuf[rows, at_rows(u)].astype(jnp.float32)
            nbuf[rows, at_rows(u)] = (x * inv * gcol[rows, :]).astype(jnp.bfloat16)
            return c

        lax.fori_loop(0, 8, norm, 0)
        r = project(u, 0)
        live = rows_of(u, CH, HD) < total
        key = jnp.where(live, finish(r[:, :HD], kg_ref[...], u), 0.0).astype(jnp.bfloat16)
        val = jnp.where(live, r[:, HD:], 0.0).astype(jnp.bfloat16)
        kbuf[at_rows(u), :] = key
        vbuf[at_rows(u), pl.ds(0, HD)] = val
        cacheb[at_rows(u), :] = jnp.where(core == 0, key, val)
        cache_out(u).start()
        return c

    def do_q(u, pair):
        r = project(u, pl.multiple_of(2 * HD + pair * 2 * HD, 2 * HD))
        q = jnp.concatenate(
            [finish(r[:, h * HD:(h + 1) * HD], qg_ref[...], u).astype(jnp.bfloat16) for h in range(2)],
            axis=0,
        )

        def attend(n):
            rows = rows_of(u, CH, n)
            start = starts_of(rows_of(u, CH, HD))[:, :1]
            keys = lax.broadcasted_iota(jnp.int32, (CH, n), 1)
            allowed = (keys >= start) & (keys <= rows)
            s = lax.dot_general(
                q, kbuf[:n, :], (((1,), (1,)), ((), ())), preferred_element_type=jnp.float32
            )
            p = jnp.exp2(s * (LOG2E / math.sqrt(HD)))
            p = jnp.concatenate(
                [jnp.where(allowed, p[h * CH:(h + 1) * CH], 0.0) for h in range(2)], axis=0
            ).astype(jnp.bfloat16)
            a = jnp.dot(p, vbuf[:n, :], preferred_element_type=jnp.float32)
            out = (a[:, :HD] / a[:, HD:]).astype(jnp.bfloat16)
            for h in range(2):
                cols = pl.ds(pl.multiple_of((pair * 2 + h) * HD, HD), HD)
                ctxb[at_rows(u), cols] = out[h * CH:(h + 1) * CH]

        lax.switch(u // 2, [functools.partial(attend, KTILE * (b + 1)) for b in range(ROWS // KTILE)])
        ctx_out(u, pair).start()

    def do_q01(u, c):
        do_q(u, 0)
        return c

    def do_q23(u, c):
        do_q(u, 1)
        return c

    def stage(k, lo, hi, fn):
        @pl.when((k >= lo) & (k < hi))
        def _():
            fn(k)

    def w_step(k):
        stage(k + LEAD, LEAD, NW, w_ahead)
        stage(k + LEAD, LEAD, NW, w0)
        stage(k, 0, NW, w1)
        stage(k - 1, 0, NW, w2)
        stage(k - 2, 0, NW, w3)
        stage(k - 3, 0, NW, w4)

    def tick(k, c):
        stage(k + LEAD, LEAD, NCH, a_ahead)
        stage(k + LEAD, LEAD, NCH, a0)
        stage(k, 0, NCH, a1)
        stage(k - 1, 0, NCH, a2)
        stage(k - 2, 0, NCH, a3)
        first_step = k + (k + 3) // 4
        w_step(first_step)

        @pl.when(lax.rem(k, 4) == 0)
        def _():
            w_step(first_step + 1)

        stage(k - 3, 0, NCH, a4)

        @pl.when(k == 0)
        def _():
            kbuf[...] = jnp.zeros_like(kbuf)
            vbuf[:, :HD] = jnp.zeros((ROWS, HD), jnp.bfloat16)
            vbuf[:, HD:] = jnp.ones((ROWS, HD), jnp.bfloat16)

        @pl.when(k == 1)
        def _():
            lax.fori_loop(0, 16 * FEAT // HD, gain_column, 0)

        @pl.when(k < NCH)
        def _():
            trig(k, 0)

        @pl.when(k == T_KV)
        def _():
            v = ss.at[pl.ds(0, 15)]
            rcopy(v, v, ss_s, ss_r, twin).wait_recv()
            sums = jnp.sum(ss[...], axis=0)
            tinv[...] = lax.rsqrt(sums * (1.0 / (16 * FEAT)) + EPS)

        last = k - 3
        for first, fn in ((T_KV, do_kv), (T_Q01, do_q01), (T_Q23, do_q23)):

            @pl.when(k >= first)
            def _():
                lax.fori_loop(jnp.where(k == first, 0, last), last + 1, fn, 0)

        return c

    lax.fori_loop(0, NCH + 3, tick, 0)

    v = ss.at[pl.ds(0, 15)]
    rcopy(v, v, ss_s, ss_r, twin).wait_send()

    def w_sent(i, c):
        v = wbuf.at[pl.ds(0, 7 * KH), pl.ds(0, HD)]
        rcopy(v, v, w_s.at[i], w_r.at[i, 0], twin).wait_send()

        return c

    def kv_sent(i, c):
        v = wbuf.at[pl.ds(0, 15 * KH), pl.ds(0, HD)]
        rcopy(v, v, w_s.at[i], w_r.at[i, 0], twin).wait_send()
        return c

    lax.fori_loop(0, 2, kv_sent, 0)
    lax.fori_loop(2, NW, w_sent, 0)

    def a_sent(i, c):
        v = xbuf.at[pl.ds(0, 15 * FEAT), pl.ds(0, CH)]
        rcopy(v, v, a_s.at[i], a_r.at[i, 0], twin).wait_send()
        return c

    lax.fori_loop(0, NCH, a_sent, 0)
    pltpu.make_async_copy(cacheb, cache_ref, out_s.at[0]).wait()
    pltpu.make_async_copy(ctxb, ctx_ref, out_s.at[1]).wait()


def hand_on(cache_in, ctx_in, cache_ref, ctx_ref, cache_held, ctx_held, sem):
    parts = []
    for n in range(4):
        rows = pl.ds(n * ROWS // 4, ROWS // 4)
        for a, (src, held, dst) in enumerate(((cache_in, cache_held, cache_ref), (ctx_in, ctx_held, ctx_ref))):
            parts.append(
                (
                    pltpu.make_async_copy(src.at[rows, :], held.at[rows, :], sem.at[n, a, 0]),
                    pltpu.make_async_copy(held.at[rows, :], dst.at[rows, :], sem.at[n, a, 1]),
                )
            )
    for fetch, _ in parts:
        fetch.start()
    for fetch, store in parts:
        fetch.wait()
        store.start()
    for _, store in parts:
        store.wait()


def per_device(activations, norm_gain, query_gain, key_gain, query_weight, keyval_weight, lengths):
    half = np.arange(64, dtype=np.float64)
    freq = np.exp(half * (-2.0 * math.log(THETA) / HD)).astype(np.float32)
    freq = jnp.asarray(np.concatenate([freq, freq])[None, :])
    vmem = pl.BlockSpec(memory_space=pltpu.VMEM)
    hbm = pl.BlockSpec(memory_space=pl.ANY)
    dma = pltpu.SemaphoreType.DMA
    bf16, f32 = jnp.bfloat16, jnp.float32
    cache, context = pl.pallas_call(
        kernel,
        out_shape=(
            jax.ShapeDtypeStruct((ROWS, HD), bf16),
            jax.ShapeDtypeStruct((ROWS, 4 * HD), bf16),
        ),
        in_specs=[pl.BlockSpec(memory_space=pltpu.SMEM)] + [vmem] * 5 + [hbm] * 2,
        out_specs=(hbm, hbm),
        scratch_shapes=[
            pltpu.VMEM((16 * FEAT, ROWS), bf16),
            pltpu.VMEM((16 * FEAT, ROWS), bf16),
            pltpu.VMEM((8 * WROWS, 6 * HD), bf16),
            pltpu.VMEM((16 * FEAT, HD), f32),
            pltpu.VMEM((16, 16, CH), f32),
            pltpu.VMEM((16, CH), f32),
            pltpu.VMEM((ROWS, HD), f32),
            pltpu.VMEM((ROWS, HD), f32),
            pltpu.VMEM((ROWS, HD), bf16),
            pltpu.VMEM((ROWS, 2 * HD), bf16),
            pltpu.VMEM((ROWS, HD), bf16),
            pltpu.VMEM((ROWS, 4 * HD), bf16),
            dma((2,)), dma, dma, dma((2,)),
            dma((NCH,)), dma((NCH, 6)), dma((NW,)), dma((NW, 6)),
        ],
        compiler_params=pltpu.CompilerParams(
            collective_id=0, has_side_effects=True, vmem_limit_bytes=56 * 2**20
        ),
        cost_estimate=pl.CostEstimate(
            flops=2 * ROWS * 5120 * 768, bytes_accessed=4 * 2**20, transcendentals=4 * ROWS * ROWS
        ),
    )(
        lengths,
        activations.T,
        norm_gain[None, :],
        freq,
        query_gain[None, :],
        key_gain[None, :],
        query_weight,
        keyval_weight,
    )
    return pl.pallas_call(
        hand_on,
        out_shape=(
            jax.ShapeDtypeStruct((ROWS, HD), bf16),
            jax.ShapeDtypeStruct((ROWS, 4 * HD), bf16),
        ),
        in_specs=[hbm] * 2,
        out_specs=(hbm, hbm),
        scratch_shapes=[
            pltpu.VMEM((ROWS, HD), bf16),
            pltpu.VMEM((ROWS, 4 * HD), bf16),
            dma((4, 2, 2)),
        ],
        compiler_params=pltpu.CompilerParams(vmem_limit_bytes=60 * 2**20),
    )(cache, context)


def solution(mesh):
    placed = (P("grp", "tp"), P(), P(), P(), P("grp", "tp"), P("grp", "tp"), P())
    return jax.shard_map(
        per_device,
        mesh=mesh,
        in_specs=placed,
        out_specs=(P("grp", "tp"), P("grp", "tp")),
        check_vma=False,
    )
```

time: 180 us -> 120 us (0.67)
  Pallas kernels: 177 us -> 119 us
  local copies, waits for them, and re-layouts: 2.34 us -> 0 us
    pallas_call x1, Pallas kernels: 60.7 us -> 2.43 us  [per_device(): pl.pallas_call(hand_on, out_shape=(jax.ShapeDtypeStruct((ROWS, HD), bf16)...]
    unnamed x1 -> x0, local copies, waits for them, and re-layouts: 2.34 us -> none
where the time goes in v3:
time: 120 us
  Pallas kernels  119 us (99%)
    pallas_call x1, Pallas kernels, per_device(): pl.pallas_call(kernel, out_shape=(jax.ShapeDtypeStruct((ROWS, HD), bf16),...  117 us
    pallas_call x1, Pallas kernels, per_device(): pl.pallas_call(hand_on, out_shape=(jax.ShapeDtypeStruct((ROWS, HD), bf16)...  2.43 us

profile of v3, /device:TPU:0, one launch (start us, length us, event | category | flops | bytes accessed | tf_op | source)
XLA Modules:
  0.0 120.0 jit_solution(15862323362437143380)
XLA Ops:
  0.6 116.9 %shard_map.95 = (bf16[1536,128]{1,0:T(8,128)(2,1)}, bf16[1536,512]{1,0:T(8,128)(2,1)}) custom-call(s32[8,8]{1,0:T(8,128)} %len_ref.1, bf16[320,1536]{1,0:T(8,128)(2,1)} %bitcast.4, f32[1,5120]{1,0:T(1,128)} %bitcast.5, f32[1,128]{1,0:T(1,128)} %constant.2.clone.freq_ref, f32[1,128]{1,0:T(1,128)} %bitcast.6, f32[1,128]{1,0:T(1,128)} %bitcast.7, ...), custom_call_target="tpu_custom_call" | custom-call | flops 12079595520 | bytes 4194304 | tf_op jit(solution)/shard_map/pallas_call | solution.py:502
  117.6 2.4 %shard_map.96 = (bf16[1536,128]{1,0:T(8,128)(2,1)}, bf16[1536,512]{1,0:T(8,128)(2,1)}) custom-call(bf16[1536,128]{1,0:T(8,128)(2,1)} %get-tuple-element.4.cache_in, bf16[1536,512]{1,0:T(8,128)(2,1)} %get-tuple-element.5.ctx_in), custom_call_target="tpu_custom_call" | custom-call | tf_op jit(solution)/shard_map/pallas_call | solution.py:542

commit v4 on v3

--- a/solution.py
+++ b/solution.py
@@ -21,7 +21,12 @@
 KH = 320
 NW = 10
 KTILE = 256
-T_KV, T_Q01, T_Q23 = 3, 5, 8
+LAG = 5
+UNIT = 2 * CH
+TASKS = (
+    (8, 0, 0), (9, 0, 1), (10, 0, 2), (12, 0, 3), (12, 1, 0), (12, 1, 1), (13, 1, 2), (13, 1, 3),
+    (14, 0, 4), (15, 1, 4), (16, 0, 5), (16, 1, 5),
+)
 LEAD = 3
 LOG2E = math.log2(math.e)
 
@@ -170,7 +175,7 @@
         w_z(i, 0, 1, g).start()
 
     def mixed(i):
-        return (i >= 2) & (lax.rem(i, 2) == 0)
+        return i < 0
 
     def w_f(i, n, owner):
         return wmsg(owner, i, w_s.at[i], w_r.at[i, (2, 2, 4)[n]], wacross)
@@ -308,14 +313,14 @@
     def at_rows(u):
         return pl.ds(pl.multiple_of(u * CH, CH), CH)
 
-    def finish(a, gains, u):
+    def finish(a, gains, rows):
         m = jnp.mean(a * a, axis=1, keepdims=True)
         a = a * lax.rsqrt(m + EPS) * gains
-        return a * cosb[at_rows(u), :] + pltpu.roll(a, HD // 2, 1) * sinb[at_rows(u), :]
-
-    def project(u, col):
+        return a * cosb[rows, :] + pltpu.roll(a, HD // 2, 1) * sinb[rows, :]
+
+    def project(rows, col):
         return lax.dot_general(
-            nbuf[:, at_rows(u)],
+            nbuf[:, rows],
             wbuf[:, pl.ds(col, 2 * HD)],
             (((0,), (0,)), ((), ())),
             preferred_element_type=jnp.float32,
@@ -324,9 +329,12 @@
     def cache_out(u):
         return pltpu.make_async_copy(cacheb.at[at_rows(u), :], cache_ref.at[at_rows(u), :], out_s.at[0])
 
+    def unit_rows(u):
+        return pl.ds(pl.multiple_of(u * UNIT, UNIT), UNIT)
+
     def ctx_out(u, pair):
         cols = pl.ds(pl.multiple_of(pair * 2 * HD, 2 * HD), 2 * HD)
-        return pltpu.make_async_copy(ctxb.at[at_rows(u), cols], ctx_ref.at[at_rows(u), cols], out_s.at[1])
+        return pltpu.make_async_copy(ctxb.at[unit_rows(u), cols], ctx_ref.at[unit_rows(u), cols], out_s.at[1])
 
     def do_kv(u, c):
         inv = tinv[pl.ds(u, 1), :]
@@ -338,9 +346,9 @@
             return c
 
         lax.fori_loop(0, 8, norm, 0)
-        r = project(u, 0)
+        r = project(at_rows(u), 0)
         live = rows_of(u, CH, HD) < total
-        key = jnp.where(live, finish(r[:, :HD], kg_ref[...], u), 0.0).astype(jnp.bfloat16)
+        key = jnp.where(live, finish(r[:, :HD], kg_ref[...], at_rows(u)), 0.0).astype(jnp.bfloat16)
         val = jnp.where(live, r[:, HD:], 0.0).astype(jnp.bfloat16)
         kbuf[at_rows(u), :] = key
         vbuf[at_rows(u), pl.ds(0, HD)] = val
@@ -349,39 +357,32 @@
         return c
 
     def do_q(u, pair):
-        r = project(u, pl.multiple_of(2 * HD + pair * 2 * HD, 2 * HD))
-        q = jnp.concatenate(
-            [finish(r[:, h * HD:(h + 1) * HD], qg_ref[...], u).astype(jnp.bfloat16) for h in range(2)],
-            axis=0,
-        )
+        r = project(unit_rows(u), pl.multiple_of(2 * HD + pair * 2 * HD, 2 * HD))
+        q = [finish(r[:, h * HD:(h + 1) * HD], qg_ref[...], unit_rows(u)).astype(jnp.bfloat16) for h in range(2)]
 
         def attend(n):
-            rows = rows_of(u, CH, n)
-            start = starts_of(rows_of(u, CH, HD))[:, :1]
-            keys = lax.broadcasted_iota(jnp.int32, (CH, n), 1)
+            rows = u * UNIT + lax.broadcasted_iota(jnp.int32, (UNIT, n), 0)
+            start = starts_of(u * UNIT + lax.broadcasted_iota(jnp.int32, (UNIT, HD), 0))[:, :1]
+            keys = lax.broadcasted_iota(jnp.int32, (UNIT, n), 1)
             allowed = (keys >= start) & (keys <= rows)
-            s = lax.dot_general(
-                q, kbuf[:n, :], (((1,), (1,)), ((), ())), preferred_element_type=jnp.float32
-            )
-            p = jnp.exp2(s * (LOG2E / math.sqrt(HD)))
-            p = jnp.concatenate(
-                [jnp.where(allowed, p[h * CH:(h + 1) * CH], 0.0) for h in range(2)], axis=0
-            ).astype(jnp.bfloat16)
-            a = jnp.dot(p, vbuf[:n, :], preferred_element_type=jnp.float32)
-            out = (a[:, :HD] / a[:, HD:]).astype(jnp.bfloat16)
             for h in range(2):
+                s = lax.dot_general(
+                    q[h], kbuf[:n, :], (((1,), (1,)), ((), ())), preferred_element_type=jnp.float32
+                )
+                p = jnp.where(allowed, jnp.exp2(s * (LOG2E / math.sqrt(HD))), 0.0).astype(jnp.bfloat16)
+                a = jnp.dot(p, vbuf[:n, :], preferred_element_type=jnp.float32)
                 cols = pl.ds(pl.multiple_of((pair * 2 + h) * HD, HD), HD)
-                ctxb[at_rows(u), cols] = out[h * CH:(h + 1) * CH]
-
-        lax.switch(u // 2, [functools.partial(attend, KTILE * (b + 1)) for b in range(ROWS // KTILE)])
+                ctxb[unit_rows(u), cols] = (a[:, :HD] / a[:, HD:]).astype(jnp.bfloat16)
+
+        lax.switch(u, [functools.partial(attend, UNIT * (b + 1)) for b in range(ROWS // UNIT)])
         ctx_out(u, pair).start()
 
-    def do_q01(u, c):
-        do_q(u, 0)
-        return c
-
-    def do_q23(u, c):
-        do_q(u, 1)
+    def do_task(n, c):
+        unit, pair = 0, 0
+        for m, (_, p, u) in enumerate(TASKS):
+            unit = jnp.where(n == m, u, unit)
+            pair = jnp.where(n == m, p, pair)
+        do_q(unit, pair)
         return c
 
     def stage(k, lo, hi, fn):
@@ -393,24 +394,17 @@
         stage(k + LEAD, LEAD, NW, w_ahead)
         stage(k + LEAD, LEAD, NW, w0)
         stage(k, 0, NW, w1)
-        stage(k - 1, 0, NW, w2)
-        stage(k - 2, 0, NW, w3)
-        stage(k - 3, 0, NW, w4)
+        stage(k - 2, 0, NW, w2)
+        stage(k - 4, 0, NW, w3)
+        stage(k - 4, 0, NW, w4)
 
     def tick(k, c):
         stage(k + LEAD, LEAD, NCH, a_ahead)
         stage(k + LEAD, LEAD, NCH, a0)
         stage(k, 0, NCH, a1)
-        stage(k - 1, 0, NCH, a2)
-        stage(k - 2, 0, NCH, a3)
-        first_step = k + (k + 3) // 4
-        w_step(first_step)
-
-        @pl.when(lax.rem(k, 4) == 0)
-        def _():
-            w_step(first_step + 1)
-
-        stage(k - 3, 0, NCH, a4)
+        stage(k - 2, 0, NCH, a2)
+        stage(k - 4, 0, NCH, a3)
+        stage(k - 5, 0, NCH, a4)
 
         @pl.when(k == 0)
         def _():
@@ -426,23 +420,28 @@
         def _():
             trig(k, 0)
 
-        @pl.when(k == T_KV)
+        @pl.when(k == LAG)
         def _():
             v = ss.at[pl.ds(0, 15)]
             rcopy(v, v, ss_s, ss_r, twin).wait_recv()
             sums = jnp.sum(ss[...], axis=0)
             tinv[...] = lax.rsqrt(sums * (1.0 / (16 * FEAT)) + EPS)
 
-        last = k - 3
-        for first, fn in ((T_KV, do_kv), (T_Q01, do_q01), (T_Q23, do_q23)):
-
-            @pl.when(k >= first)
-            def _():
-                lax.fori_loop(jnp.where(k == first, 0, last), last + 1, fn, 0)
-
-        return c
-
-    lax.fori_loop(0, NCH + 3, tick, 0)
+        @pl.when(k >= LAG)
+        def _():
+            do_kv(k - LAG, 0)
+
+        @pl.when(k == 0)
+        def _():
+            w_step(0)
+
+        w_step(k + 1)
+        before = sum(jnp.where(k > task[0], 1, 0) for task in TASKS)
+        after = sum(jnp.where(k >= task[0], 1, 0) for task in TASKS)
+        lax.fori_loop(before, after, do_task, 0)
+        return c
+
+    lax.fori_loop(0, NCH + LAG, tick, 0)
 
     v = ss.at[pl.ds(0, 15)]
     rcopy(v, v, ss_s, ss_r, twin).wait_send()

time: 120 us -> 100 us (0.83)
  Pallas kernels: 119 us -> 98.4 us
    pallas_call x1, Pallas kernels: 117 us -> 96 us  [per_device(): pl.pallas_call(kernel, out_shape=(jax.ShapeDtypeStruct((ROWS, HD), bf16),...]
where the time goes in v4:
time: 100 us; the launch traced here: 99.1 us
  Pallas kernels  98.4 us (98%)
    pallas_call x1, Pallas kernels, per_device(): pl.pallas_call(kernel, out_shape=(jax.ShapeDtypeStruct((ROWS, HD), bf16),...  96 us
    pallas_call x1, Pallas kernels, per_device(): pl.pallas_call(hand_on, out_shape=(jax.ShapeDtypeStruct((ROWS, HD), bf16)...  2.43 us

profile of v4, /device:TPU:0, one launch (start us, length us, event | category | flops | bytes accessed | tf_op | source)
XLA Modules:
  0.0 99.1 jit_solution(18378313615697311708)
XLA Ops:
  0.6 96.0 %shard_map.95 = (bf16[1536,128]{1,0:T(8,128)(2,1)}, bf16[1536,512]{1,0:T(8,128)(2,1)}) custom-call(s32[8,8]{1,0:T(8,128)} %len_ref.1, bf16[320,1536]{1,0:T(8,128)(2,1)} %bitcast.4, f32[1,5120]{1,0:T(1,128)} %bitcast.5, f32[1,128]{1,0:T(1,128)} %constant.2.clone.freq_ref, f32[1,128]{1,0:T(1,128)} %bitcast.6, f32[1,128]{1,0:T(1,128)} %bitcast.7, ...), custom_call_target="tpu_custom_call" | custom-call | flops 12079595520 | bytes 4194304 | tf_op jit(solution)/shard_map/pallas_call | solution.py:501
  96.6 2.4 %shard_map.96 = (bf16[1536,128]{1,0:T(8,128)(2,1)}, bf16[1536,512]{1,0:T(8,128)(2,1)}) custom-call(bf16[1536,128]{1,0:T(8,128)(2,1)} %get-tuple-element.4.cache_in, bf16[1536,512]{1,0:T(8,128)(2,1)} %get-tuple-element.5.ctx_in), custom_call_target="tpu_custom_call" | custom-call | tf_op jit(solution)/shard_map/pallas_call | solution.py:541

commit v5 on v4

--- a/solution.py
+++ b/solution.py
@@ -24,8 +24,8 @@
 LAG = 5
 UNIT = 2 * CH
 TASKS = (
-    (8, 0, 0), (9, 0, 1), (10, 0, 2), (12, 0, 3), (12, 1, 0), (12, 1, 1), (13, 1, 2), (13, 1, 3),
-    (14, 0, 4), (15, 1, 4), (16, 0, 5), (16, 1, 5),
+    (9, 0, 2, 0), (9, 0, 2, 1), (10, 0, 2, 2), (11, 2, 2, 0), (12, 2, 2, 1),
+    (12, 2, 2, 2), (13, 0, 4, 3), (14, 0, 4, 4), (16, 0, 4, 5),
 )
 LEAD = 3
 LOG2E = math.log2(math.e)
@@ -34,7 +34,7 @@
 def kernel(
     len_ref, x_ref, gain_ref, freq_ref, qg_ref, kg_ref, wq_ref, wkv_ref,
     cache_ref, ctx_ref,
-    xbuf, nbuf, wbuf, gcol, ss, tinv, cosb, sinb, kbuf, vbuf, cacheb, ctxb,
+    xbuf, nbuf, wbuf, gcol, ss, tinv, startb, cosb, sinb, kbuf, vbuf, cacheb, ctxb,
     out_s, ss_s, ss_r, loc_s, a_s, a_r, w_s, w_r,
 ):
     g = lax.axis_index("grp")
@@ -106,9 +106,11 @@
 
     def trig(u, c):
         rows = rows_of(u, CH, HD)
-        angle = (rows - starts_of(rows)).astype(jnp.float32) * freq_ref[...]
+        start = starts_of(rows)
+        angle = (rows - start).astype(jnp.float32) * freq_ref[...]
         lane = lax.broadcasted_iota(jnp.int32, (CH, HD), 1)
         at = pl.ds(pl.multiple_of(u * CH, CH), CH)
+        startb[at, :] = start
         cosb[at, :] = jnp.cos(angle)
         sinb[at, :] = jnp.where(lane < HD // 2, -1.0, 1.0) * jnp.sin(angle)
         return c
@@ -318,10 +320,10 @@
         a = a * lax.rsqrt(m + EPS) * gains
         return a * cosb[rows, :] + pltpu.roll(a, HD // 2, 1) * sinb[rows, :]
 
-    def project(rows, col):
+    def project(rows, col, n):
         return lax.dot_general(
             nbuf[:, rows],
-            wbuf[:, pl.ds(col, 2 * HD)],
+            wbuf[:, pl.ds(col, n)],
             (((0,), (0,)), ((), ())),
             preferred_element_type=jnp.float32,
         )
@@ -332,8 +334,8 @@
     def unit_rows(u):
         return pl.ds(pl.multiple_of(u * UNIT, UNIT), UNIT)
 
-    def ctx_out(u, pair):
-        cols = pl.ds(pl.multiple_of(pair * 2 * HD, 2 * HD), 2 * HD)
+    def ctx_out(u, first, heads):
+        cols = pl.ds(pl.multiple_of(first * HD, HD), heads * HD)
         return pltpu.make_async_copy(ctxb.at[unit_rows(u), cols], ctx_ref.at[unit_rows(u), cols], out_s.at[1])
 
     def do_kv(u, c):
@@ -346,7 +348,7 @@
             return c
 
         lax.fori_loop(0, 8, norm, 0)
-        r = project(at_rows(u), 0)
+        r = project(at_rows(u), 0, 2 * HD)
         live = rows_of(u, CH, HD) < total
         key = jnp.where(live, finish(r[:, :HD], kg_ref[...], at_rows(u)), 0.0).astype(jnp.bfloat16)
         val = jnp.where(live, r[:, HD:], 0.0).astype(jnp.bfloat16)
@@ -356,33 +358,42 @@
         cache_out(u).start()
         return c
 
-    def do_q(u, pair):
-        r = project(unit_rows(u), pl.multiple_of(2 * HD + pair * 2 * HD, 2 * HD))
-        q = [finish(r[:, h * HD:(h + 1) * HD], qg_ref[...], unit_rows(u)).astype(jnp.bfloat16) for h in range(2)]
+    def do_q(heads, units, u, first):
+        r = project(unit_rows(u), pl.multiple_of((2 + first) * HD, HD), heads * HD)
+        q = [
+            finish(r[:, h * HD:(h + 1) * HD], qg_ref[...], unit_rows(u)).astype(jnp.bfloat16)
+            for h in range(heads)
+        ]
 
         def attend(n):
             rows = u * UNIT + lax.broadcasted_iota(jnp.int32, (UNIT, n), 0)
-            start = starts_of(u * UNIT + lax.broadcasted_iota(jnp.int32, (UNIT, HD), 0))[:, :1]
+            start = startb[unit_rows(u), :1]
             keys = lax.broadcasted_iota(jnp.int32, (UNIT, n), 1)
             allowed = (keys >= start) & (keys <= rows)
-            for h in range(2):
+            for h in range(heads):
                 s = lax.dot_general(
                     q[h], kbuf[:n, :], (((1,), (1,)), ((), ())), preferred_element_type=jnp.float32
                 )
                 p = jnp.where(allowed, jnp.exp2(s * (LOG2E / math.sqrt(HD))), 0.0).astype(jnp.bfloat16)
                 a = jnp.dot(p, vbuf[:n, :], preferred_element_type=jnp.float32)
-                cols = pl.ds(pl.multiple_of((pair * 2 + h) * HD, HD), HD)
+                cols = pl.ds(pl.multiple_of((first + h) * HD, HD), HD)
                 ctxb[unit_rows(u), cols] = (a[:, :HD] / a[:, HD:]).astype(jnp.bfloat16)
 
-        lax.switch(u, [functools.partial(attend, UNIT * (b + 1)) for b in range(ROWS // UNIT)])
-        ctx_out(u, pair).start()
+        lax.switch(u - units[0], [functools.partial(attend, UNIT * (b + 1)) for b in units])
+        ctx_out(u, first, heads).start()
 
     def do_task(n, c):
-        unit, pair = 0, 0
-        for m, (_, p, u) in enumerate(TASKS):
+        unit, first, heads = 0, 0, 0
+        for m, (_, f, h, u) in enumerate(TASKS):
             unit = jnp.where(n == m, u, unit)
-            pair = jnp.where(n == m, p, pair)
-        do_q(unit, pair)
+            first = jnp.where(n == m, f, first)
+            heads = jnp.where(n == m, h // 4, heads)
+        lax.switch(
+            heads,
+            [functools.partial(do_q, h, us) for h, us in ((2, range(4)), (4, range(2, 6)))],
+            unit,
+            first,
+        )
         return c
 
     def stage(k, lo, hi, fn):
@@ -394,8 +405,11 @@
         stage(k + LEAD, LEAD, NW, w_ahead)
         stage(k + LEAD, LEAD, NW, w0)
         stage(k, 0, NW, w1)
-        stage(k - 2, 0, NW, w2)
-        stage(k - 4, 0, NW, w3)
+        stage(k - 2, 0, NW - 1, w2)
+        stage(k - 1, NW - 1, NW, w2)
+        stage(k - 4, 0, NW - 2, w3)
+        stage(k - 3, NW - 2, NW - 1, w3)
+        stage(k - 2, NW - 1, NW, w3)
         stage(k - 4, 0, NW, w4)
 
     def tick(k, c):
@@ -416,9 +430,9 @@
         def _():
             lax.fori_loop(0, 16 * FEAT // HD, gain_column, 0)
 
-        @pl.when(k < NCH)
-        def _():
-            trig(k, 0)
+        @pl.when(k < NCH // 2)
+        def _():
+            lax.fori_loop(2 * k, 2 * k + 2, trig, 0)
 
         @pl.when(k == LAG)
         def _():
@@ -427,15 +441,12 @@
             sums = jnp.sum(ss[...], axis=0)
             tinv[...] = lax.rsqrt(sums * (1.0 / (16 * FEAT)) + EPS)
 
+        w_step(k)
+
         @pl.when(k >= LAG)
         def _():
             do_kv(k - LAG, 0)
 
-        @pl.when(k == 0)
-        def _():
-            w_step(0)
-
-        w_step(k + 1)
         before = sum(jnp.where(k > task[0], 1, 0) for task in TASKS)
         after = sum(jnp.where(k >= task[0], 1, 0) for task in TASKS)
         lax.fori_loop(before, after, do_task, 0)
@@ -513,6 +524,7 @@
             pltpu.VMEM((16 * FEAT, HD), f32),
             pltpu.VMEM((16, 16, CH), f32),
             pltpu.VMEM((16, CH), f32),
+            pltpu.VMEM((ROWS, HD), jnp.int32),
             pltpu.VMEM((ROWS, HD), f32),
             pltpu.VMEM((ROWS, HD), f32),
             pltpu.VMEM((ROWS, HD), bf16),

time: 100 us -> 98.9 us (0.989)
  Pallas kernels: 98.4 us -> 97.3 us
    pallas_call x1, Pallas kernels: 96 us -> 94.9 us  [per_device(): pl.pallas_call(kernel, out_shape=(jax.ShapeDtypeStruct((ROWS, HD), bf16),...]
where the time goes in v5:
time: 98.9 us; the launch traced here: 98 us
  Pallas kernels  97.3 us (98%)
    pallas_call x1, Pallas kernels, per_device(): pl.pallas_call(kernel, out_shape=(jax.ShapeDtypeStruct((ROWS, HD), bf16),...  94.9 us
    pallas_call x1, Pallas kernels, per_device(): pl.pallas_call(hand_on, out_shape=(jax.ShapeDtypeStruct((ROWS, HD), bf16)...  2.43 us

profile of v5, /device:TPU:0, one launch (start us, length us, event | category | flops | bytes accessed | tf_op | source)
XLA Modules:
  0.0 98.0 jit_solution(16987740069287150583)
XLA Ops:
  0.6 94.9 %shard_map.95 = (bf16[1536,128]{1,0:T(8,128)(2,1)}, bf16[1536,512]{1,0:T(8,128)(2,1)}) custom-call(s32[8,8]{1,0:T(8,128)} %len_ref.1, bf16[320,1536]{1,0:T(8,128)(2,1)} %bitcast.4, f32[1,5120]{1,0:T(1,128)} %bitcast.5, f32[1,128]{1,0:T(1,128)} %constant.2.clone.freq_ref, f32[1,128]{1,0:T(1,128)} %bitcast.6, f32[1,128]{1,0:T(1,128)} %bitcast.7, ...), custom_call_target="tpu_custom_call" | custom-call | flops 12079595520 | bytes 4194304 | tf_op jit(solution)/shard_map/pallas_call | solution.py:512
  95.6 2.4 %shard_map.96 = (bf16[1536,128]{1,0:T(8,128)(2,1)}, bf16[1536,512]{1,0:T(8,128)(2,1)}) custom-call(bf16[1536,128]{1,0:T(8,128)(2,1)} %get-tuple-element.4.cache_in, bf16[1536,512]{1,0:T(8,128)(2,1)} %get-tuple-element.5.ctx_in), custom_call_target="tpu_custom_call" | custom-call | tf_op jit(solution)/shard_map/pallas_call | solution.py:553

commit v6 on v5

--- a/solution.py
+++ b/solution.py
@@ -329,7 +329,7 @@
         )
 
     def cache_out(u):
-        return pltpu.make_async_copy(cacheb.at[at_rows(u), :], cache_ref.at[at_rows(u), :], out_s.at[0])
+        return pltpu.make_async_copy(cacheb.at[unit_rows(u), :], cache_ref.at[unit_rows(u), :], out_s.at[0])
 
     def unit_rows(u):
         return pl.ds(pl.multiple_of(u * UNIT, UNIT), UNIT)
@@ -348,14 +348,20 @@
             return c
 
         lax.fori_loop(0, 8, norm, 0)
-        r = project(at_rows(u), 0, 2 * HD)
-        live = rows_of(u, CH, HD) < total
-        key = jnp.where(live, finish(r[:, :HD], kg_ref[...], at_rows(u)), 0.0).astype(jnp.bfloat16)
-        val = jnp.where(live, r[:, HD:], 0.0).astype(jnp.bfloat16)
-        kbuf[at_rows(u), :] = key
-        vbuf[at_rows(u), pl.ds(0, HD)] = val
-        cacheb[at_rows(u), :] = jnp.where(core == 0, key, val)
-        cache_out(u).start()
+
+        @pl.when(lax.rem(u, 2) == 1)
+        def _():
+            n = u // 2
+            rows = unit_rows(n)
+            r = project(rows, 0, 2 * HD)
+            live = n * UNIT + lax.broadcasted_iota(jnp.int32, (UNIT, HD), 0) < total
+            key = jnp.where(live, finish(r[:, :HD], kg_ref[...], rows), 0.0).astype(jnp.bfloat16)
+            val = jnp.where(live, r[:, HD:], 0.0).astype(jnp.bfloat16)
+            kbuf[rows, :] = key
+            vbuf[rows, pl.ds(0, HD)] = val
+            cacheb[rows, :] = jnp.where(core == 0, key, val)
+            cache_out(n).start()
+
         return c
 
     def do_q(heads, units, u, first):

time: 98.9 us -> 98.4 us (level)
  Pallas kernels: 97.3 us -> 96 us
    pallas_call x1, Pallas kernels: 94.9 us -> 93.6 us  [per_device(): pl.pallas_call(kernel, out_shape=(jax.ShapeDtypeStruct((ROWS, HD), bf16),...]
where the time goes in v6:
time: 98.4 us; the launch traced here: 96.7 us
  Pallas kernels  96 us (98%)
    pallas_call x1, Pallas kernels, per_device(): pl.pallas_call(kernel, out_shape=(jax.ShapeDtypeStruct((ROWS, HD), bf16),...  93.6 us
    pallas_call x1, Pallas kernels, per_device(): pl.pallas_call(hand_on, out_shape=(jax.ShapeDtypeStruct((ROWS, HD), bf16)...  2.43 us

profile of v6, /device:TPU:0, one launch (start us, length us, event | category | flops | bytes accessed | tf_op | source)
XLA Modules:
  0.0 96.7 jit_solution(6644594203481877769)
XLA Ops:
  0.6 93.6 %shard_map.95 = (bf16[1536,128]{1,0:T(8,128)(2,1)}, bf16[1536,512]{1,0:T(8,128)(2,1)}) custom-call(s32[8,8]{1,0:T(8,128)} %len_ref.1, bf16[320,1536]{1,0:T(8,128)(2,1)} %bitcast.4, f32[1,5120]{1,0:T(1,128)} %bitcast.5, f32[1,128]{1,0:T(1,128)} %constant.2.clone.freq_ref, f32[1,128]{1,0:T(1,128)} %bitcast.6, f32[1,128]{1,0:T(1,128)} %bitcast.7, ...), custom_call_target="tpu_custom_call" | custom-call | flops 12079595520 | bytes 4194304 | tf_op jit(solution)/shard_map/pallas_call | solution.py:518
  94.3 2.4 %shard_map.96 = (bf16[1536,128]{1,0:T(8,128)(2,1)}, bf16[1536,512]{1,0:T(8,128)(2,1)}) custom-call(bf16[1536,128]{1,0:T(8,128)(2,1)} %get-tuple-element.4.cache_in, bf16[1536,512]{1,0:T(8,128)(2,1)} %get-tuple-element.5.ctx_in), custom_call_target="tpu_custom_call" | custom-call | tf_op jit(solution)/shard_map/pallas_call | solution.py:559
